TPU v7x, 32 devices: a whole 2x2x4 slice. The times are simulated.
32 devices in a mesh: layer: 16 (over z, x, core), rep: 2 (over y).
Axes of the slice: x: 2, y: 2, z: 4, core: 2. Of those that a mesh axis runs over, the one named last changes fastest.
Arguments:
- gradients: bfloat16 [2, 16, 512, 1024], P('rep', 'layer'), may hold values from -60 to 60
- inverse_out: bfloat16 [16, 512, 512], P('layer', 'rep'), may hold values from -1 to 4
- inverse_in: bfloat16 [16, 1024, 1024], P('layer', 'rep'), may hold values from -1 to 4
- cross_out: bfloat16 [16, 512, 512], P('layer', 'rep'), may hold values from -0.125 to 0.125
- cross_in: bfloat16 [16, 1024, 1024], P('layer', 'rep'), may hold values from -0.1875 to 0.1875
- momentum: float32 [16, 512, 1024], P('layer', 'rep'), may hold values from -3 to 3
Outputs:
- momentum_new: float32 [16, 512, 1024], P('layer', 'rep')
All inputs are finite; a program needn't handle non-finite values.
Results may differ from a plain program's by a relative error of at most 0.003.
Values may be sent and summed in bfloat16 or wider, within the bound.
No kernel may reach another device: no remote copies, remote signals or barrier semaphores. Data moves between devices by JAX's collectives and lax.ppermute only.
A program may use at most 64 MiB of HBM per device.

v0:
```python
import functools

import jax
import jax.numpy as jnp
from jax import lax
from jax.experimental import pallas as pl
from jax.experimental.pallas import tpu as pltpu
from jax.sharding import PartitionSpec as P

SHARES = (2, 1, 1)
ROWS = 16
TILE = 256
HALF = jnp.bfloat16
FULL = jnp.float32


def passed_along(value, axis, steps):
    count = lax.axis_size(axis)
    initial, last = (max(0, -steps), min(count, count - steps))
    return lax.ppermute(value, axis, [(source, source + steps) for source in range(initial, last)])


def from_peers(value, axis):
    count = lax.axis_size(axis)
    return [
        lax.ppermute(value, axis, [(source, (source - step) % count) for source in range(count)])
        for step in range(1, count)
    ]


def to_peer(value, axis, step):
    count = lax.axis_size(axis)
    return lax.ppermute(
        value, axis, [(source, (source + step) % count) for source in range(count)]
    )


def dot(left, right, contract=((1,), (0,))):
    return lax.dot_general(left, right, (contract, ((), ())), preferred_element_type=FULL)


def span(me_ref, step, count, size):
    start = lax.rem(me_ref[0] + step, count) * size
    return pl.ds(pl.multiple_of(start, size), size)


def cut_kernel(widths, me, cross_out, inverse_out, inverse_in, pair, *refs):
    pieces, sems = refs[:-1], refs[-1]
    rows, start = cross_out.shape[0], 0
    copies = [
        pltpu.make_async_copy(cross_out, pair.at[:rows], sems.at[0]),
        pltpu.make_async_copy(inverse_out, pair.at[rows:], sems.at[1]),
    ]
    for at, width in enumerate(widths):
        source = inverse_in.at[:, start : start + width]
        copies.append(pltpu.make_async_copy(source, pieces[at], sems.at[2 + at]))
        start += width
    for copy in copies:
        copy.start()
    for copy in copies:
        copy.wait()


def first_kernel(count, me, following, own, *refs):
    others, out = refs[: count - 1], refs[-1]
    rows = own.shape[0]

    @pl.loop(0, out.shape[1] // TILE)
    def _(at):
        columns = pl.ds(pl.multiple_of(at * TILE, TILE), TILE)
        right = following[:, columns]
        out[span(me, 0, count, rows), columns] = dot(own[...], right).astype(HALF)
        for step in range(1, count):
            block = others[step - 1][:rows, :]
            out[span(me, step, count, rows), columns] = dot(block, right).astype(HALF)


def left_kernel(count, me, grads, first, inv_own, *refs):
    rights, others, out = refs[:count], refs[count : 2 * count - 1], refs[2 * count - 1]
    depth, rows = rights[0].shape[0], inv_own.shape[0]

    @pl.loop(0, out.shape[1] // TILE)
    def _(at):
        columns = pl.ds(pl.multiple_of(at * TILE, TILE), TILE)
        cross = sum(
            dot(first[:, span(me, step, count, depth)], rights[step][:, columns])
            for step in range(count)
        )
        residual = (grads[:, columns].astype(FULL) - cross).astype(HALF)
        out[span(me, 0, count, rows), columns] = dot(inv_own[...], residual).astype(HALF)
        for step in range(1, count):
            block = others[step - 1][rows:, :]
            out[span(me, step, count, rows), columns] = dot(block, residual).astype(HALF)


def chunk_kernel(count, me, left, cross_own, own_piece, *refs):
    pieces, others = refs[: count - 1], refs[count - 1 : 2 * count - 2]
    precond, back = refs[-2:]
    depth, rows = own_piece.shape[0], cross_own.shape[0]
    product = dot(left[:, span(me, 0, count, depth)], own_piece[...])
    for step in range(1, count):
        product += dot(left[:, span(me, step, count, depth)], pieces[step - 1][...])
    precond[...] = product.astype(HALF)
    turned = ((0,), (0,))
    result = dot(cross_own[...], precond[span(me, 0, count, rows), :], turned)
    for step in range(1, count):
        block = others[step - 1][:rows, :]
        result += dot(block, precond[span(me, step, count, rows), :], turned)
    back[...] = result.astype(HALF)


def stack(target, values, lines=slice(None)):
    start = 0
    for value in values:
        target[:, start : start + value.shape[1]] = value[lines, :]
        start += value.shape[1]


def early_kernel(count, rows, me, *refs):
    total = len(SHARES)
    preconds, backs = refs[:total], refs[total : 2 * total - 1]
    rights = refs[2 * total - 1 : 2 * total - 1 + count]
    nears, (right_last, staged, stacked) = refs[2 * total - 1 + count : -3], refs[-3:]
    depth, known, near = rights[0].shape[0], stacked.shape[1], staged.shape[0]
    for row_step in range(1, count):
        start = lax.rem(me[0] + row_step, count) * rows
        lines = pl.ds(pl.multiple_of(start, ROWS), near)
        stack(staged, preconds, lines)
        stack(stacked, backs, lines)
        for step in range(count):
            columns = span(me, step, count, depth)
            product = dot(stacked[...], rights[step][:, :known], ((1,), (1,)))
            update = staged[:, columns].astype(FULL) - product
            nears[row_step - 1][:, columns] = update.astype(HALF)
    for step in range(count):
        right_last[span(me, step, count, depth), :] = rights[step][:, known:]


def gather_kernel(count, me, *refs):
    total = len(SHARES)
    preconds, backs = refs[:total], refs[total : 2 * total - 1]
    rights = refs[2 * total - 1 : 2 * total - 1 + count]
    partial, staged, stacked = refs[2 * total - 1 + count :]
    depth, known = rights[0].shape[0], stacked.shape[1]
    stack(staged, preconds)
    stack(stacked, backs)
    for step in range(count):
        columns = span(me, step, count, depth)
        right = rights[step][:, :known]
        for row in range(0, staged.shape[0], TILE):
            here = slice(row, row + TILE)
            product = dot(stacked[here, :], right, ((1,), (1,)))
            partial[here, columns] = staged[here, columns].astype(FULL) - product


def update_kernel(count, me, partial, back, right_last, *refs):
    squares, own = refs[:2]
    fars, rests = refs[2 : count + 1], refs[count + 1 :]
    rows, wide = own.shape
    total = jnp.zeros((), FULL)
    for step in range(count):
        here = span(me, step, count, rows)
        for start in range(0, wide, TILE):
            columns = slice(start, start + TILE)
            update = partial[here, columns] - dot(
                back[here, :], right_last[columns, :], ((1,), (1,))
            )
            total += jnp.sum(update * update)
            if step == 0:
                own[:, columns] = update
            else:
                near = rows - fars[step - 1].shape[0]
                fars[step - 1][:, columns] = update[near:].astype(HALF)
        if step:
            start = lax.rem(me[0] + step, count) * rows
            lines = pl.ds(pl.multiple_of(start, ROWS), rests[step - 1].shape[0])
            rests[step - 1][...] = back[lines, :]
    squares[...] = jnp.full(squares.shape, total, FULL)


def scale_of(squares, size):
    return lax.rsqrt(squares * (1.0 / size) + 1e-06)


def final_kernel(count, size, momentum, squares, own, right_last, *refs):
    peers = count - 1
    others, nears, fars, rests = (refs[at * peers : (at + 1) * peers] for at in range(4))
    out, scratch, sems = refs[-3:]
    near = nears[0].shape[0]
    scales = [scale_of(value[0:1, 0:1], size) * (1.0 / count) for value in (squares, *others)]
    copies = []
    for part, here in enumerate((slice(0, near), slice(near, scratch.shape[0]))):
        total = own[here, :] * scales[0]
        for step in range(peers):
            if part:
                update = fars[step][...].astype(FULL)
            else:
                rest = dot(rests[step][...], right_last[...], ((1,), (1,)))
                update = nears[step][...].astype(FULL) - rest
            total += update * scales[step + 1]
        scratch[here, :] = 0.9 * momentum[here, :] + total
        copies.append(
            pltpu.make_async_copy(scratch.at[here, :], out.at[here, :], sems.at[part])
        )
        copies[-1].start()
    for copy in copies:
        copy.wait()


def call(kernel, outs, operands, flops, **options):
    moved = sum(value.size * value.dtype.itemsize for value in (*operands, *outs))
    vmem = pl.BlockSpec(memory_space=pltpu.VMEM)
    specs = [pl.BlockSpec(memory_space=pltpu.SMEM)] + [vmem] * (len(operands) - 1)
    settings = dict(in_specs=specs, out_specs=[vmem] * len(outs))
    settings.update(options)
    return pl.pallas_call(
        kernel,
        out_shape=outs,
        compiler_params=pltpu.CompilerParams(vmem_limit_bytes=16 * 1024 * 1024),
        cost_estimate=pl.CostEstimate(flops=flops, bytes_accessed=moved // 64, transcendentals=0),
        **settings,
    )(*operands)


def body(gradients, inverse_out, inverse_in, cross_out, cross_in, momentum):
    own_block = gradients[0, 0]
    tall, wide = own_block.shape
    count = lax.axis_size("rep")
    me = lax.axis_index("rep").astype(jnp.int32).reshape(1)
    widths = [share * wide // sum(SHARES) for share in SHARES]
    rows = momentum.shape[1]
    shape = jax.ShapeDtypeStruct
    part = functools.partial

    anywhere = pl.BlockSpec(memory_space=pl.ANY)
    out_rows, out_wide = cross_out.shape[1:]
    pair, *cuts = call(
        part(cut_kernel, widths),
        [shape((2 * out_rows, out_wide), HALF)]
        + [shape((inverse_in.shape[1], width), HALF) for width in widths],
        [me, cross_out[0], inverse_out[0], inverse_in[0]],
        0,
        in_specs=[pl.BlockSpec(memory_space=pltpu.SMEM)] + [anywhere] * 3,
        scratch_shapes=[pltpu.SemaphoreType.DMA((2 + len(widths),))],
    )
    pairs = from_peers(pair, "rep")
    in_blocks = [cross_in[0], *from_peers(cross_in[0], "rep")]
    following = passed_along(own_block, "layer", -1)

    cut_peers = [from_peers(piece, "rep") for piece in cuts]
    (first,) = call(
        part(first_kernel, count),
        [shape((tall, wide), HALF)],
        [me, following, cross_out[0], *pairs],
        tall * tall * wide // 32,
    )
    previous_blocks = [passed_along(block, "layer", 1) for block in in_blocks]
    (left,) = call(
        part(left_kernel, count),
        [shape((tall, wide), HALF)],
        [me, own_block, first, inverse_out[0], *in_blocks, *pairs],
        tall * wide * (tall + wide) // 32,
    )
    preconds, backs = [], []
    for at, (piece, peers) in enumerate(zip(cuts, cut_peers)):
        weight = 256 if at == len(cuts) - 1 else 1
        precond, back = call(
            part(chunk_kernel, count),
            [shape((tall, piece.shape[1]), HALF)] * 2,
            [me, left, cross_out[0], piece, *peers, *pairs],
            weight * tall * piece.shape[1] * (tall + wide) // 32,
        )
        preconds.append(precond)
        backs.append(passed_along(back, "layer", 1))
    near = 5 * rows // 8 // ROWS * ROWS
    peers, last = count - 1, widths[-1]
    *nears, right_last = call(
        part(early_kernel, count, rows),
        [shape((near, wide), HALF)] * peers + [shape((wide, last), HALF)],
        [me, *preconds, *backs[:-1], *previous_blocks],
        2 * peers * near * wide * (wide - last),
        scratch_shapes=[pltpu.VMEM((near, wide), HALF), pltpu.VMEM((near, wide - last), HALF)],
    )
    nears = [to_peer(value, "rep", at + 1) for at, value in enumerate(nears)]
    (partial,) = call(
        part(gather_kernel, count),
        [shape((tall, wide), FULL)],
        [me, *preconds, *backs[:-1], *previous_blocks],
        2 * tall * wide * (wide - last),
        scratch_shapes=[pltpu.VMEM((tall, wide), HALF), pltpu.VMEM((tall, wide - last), HALF)],
    )
    squares, own, *sends = call(
        part(update_kernel, count),
        [shape((8, 128), FULL), shape((rows, wide), FULL)]
        + [shape((rows - near, wide), HALF)] * peers
        + [shape((near, last), HALF)] * peers,
        [me, partial, backs[-1], right_last],
        2 * tall * wide * last,
    )
    sends = [to_peer(value, "rep", at % peers + 1) for at, value in enumerate(sends)]
    others = [to_peer(squares, "rep", step) for step in range(1, count)]
    operands = [momentum[0], squares, own, right_last, *others, *nears, *sends]
    (result,) = call(
        part(final_kernel, count, tall * wide),
        [shape((rows, wide), FULL)],
        operands,
        4 * rows * wide,
        in_specs=[pl.BlockSpec(memory_space=pltpu.VMEM)] * len(operands),
        out_specs=[anywhere],
        scratch_shapes=[pltpu.VMEM((rows, wide), FULL), pltpu.SemaphoreType.DMA((2,))],
    )
    return result[None]


def solution(mesh):
    in_specs = (
        P("rep", "layer", None, None),
        P("layer", "rep", None),
        P("layer", "rep", None),
        P("layer", "rep", None),
        P("layer", "rep", None),
        P("layer", "rep", None),
    )
    out_specs = P("layer", "rep", None)
    return jax.shard_map(body, mesh=mesh, in_specs=in_specs, out_specs=out_specs, check_vma=False)
```

profile of v0, /device:TPU:0, one launch (start us, length us, event | category | flops | bytes accessed | tf_op | source)
XLA Modules:
  0.0 81.5 jit_solution(11482701806771275206)
XLA Ops:
  0.0 3.0 %collective-permute-start.2 = (bf16[512,1024]{1,0:T(8,128)(2,1)}, bf16[512,1024]{1,0:T(8,128)(2,1)S(1)}, u32[]{:S(2)}, u32[]{:S(2)}) collective-permute-start(bf16[512,1024]{1,0:T(8,128)(2,1)} %bitcast.18), channel_id=1, source_target_pairs={{0,1},{1,0},{2,3},{3,2},{4,5},{5,4},{6,7},{7,6},{8,9},{9,8},{10,11... | collective-permute-start | bytes 3145736 | tf_op jit(solution)/shard_map/ppermute | solution.py:26
  3.0 1.3 %collective-permute-start = (bf16[512,1024]{1,0:T(8,128)(2,1)}, bf16[512,1024]{1,0:T(8,128)(2,1)S(1)}, u32[]{:S(2)}, u32[]{:S(2)}) collective-permute-start(bf16[512,1024]{1,0:T(8,128)(2,1)} %bitcast.16), channel_id=1, source_target_pairs={{2,0},{4,2},{6,4},{8,6},{10,8},{12,10},{14,12},{16,14},{18,16},{20... | collective-permute-start | bytes 3145736 | tf_op jit(solution)/shard_map/ppermute | solution.py:20
  4.3 0.9 %copy-done = bf16[1,256,512]{2,1,0:T(8,128)(2,1)S(1)} copy-done((bf16[1,256,512]{2,1,0:T(8,128)(2,1)S(1)}, bf16[1,256,512]{2,1,0:T(8,128)(2,1)}, u32[]{:S(2)}) %copy-start) | copy-done | bytes 262168
  5.2 1.2 %copy-done.2 = bf16[1,512,1024]{2,1,0:T(8,128)(2,1)S(1)} copy-done((bf16[1,512,1024]{2,1,0:T(8,128)(2,1)S(1)}, bf16[1,512,1024]{2,1,0:T(8,128)(2,1)}, u32[]{:S(2)}) %copy-start.2) | copy-done | bytes 1048600
  6.4 0.9 %copy-done.3 = bf16[1,256,512]{2,1,0:T(8,128)(2,1)S(1)} copy-done((bf16[1,256,512]{2,1,0:T(8,128)(2,1)S(1)}, bf16[1,256,512]{2,1,0:T(8,128)(2,1)}, u32[]{:S(2)}) %copy-start.3) | copy-done | bytes 262168
  7.4 0.2 shard_map.64
  7.7 2.0 %collective-permute-start.3 = (bf16[512,512]{1,0:T(8,128)(2,1)S(1)}, bf16[512,512]{1,0:T(8,128)(2,1)S(1)}, u32[]{:S(2)}, u32[]{:S(2)}) collective-permute-start(bf16[512,512]{1,0:T(8,128)(2,1)S(1)} %get-tuple-element.22.own_piece), channel_id=1, source_target_pairs={{0,1},{1,0},{2,3},{3,2},{4,5},{5,4},{6,7},{7,6},{8,9},{9,8},{10,11... | collective-permute-start | bytes 1572872 | tf_op jit(solution)/shard_map/ppermute | solution.py:26
  9.7 2.5 %collective-permute-start.8 = (bf16[512,1024]{1,0:T(8,128)(2,1)}, bf16[512,1024]{1,0:T(8,128)(2,1)S(1)}, u32[]{:S(2)}, u32[]{:S(2)}) collective-permute-start(bf16[512,1024]{1,0:T(8,128)(2,1)} %bitcast.19), channel_id=1, source_target_pairs={{0,2},{2,4},{4,6},{6,8},{8,10},{10,12},{12,14},{14,16},{16,18},{18... | collective-permute-start | bytes 3145736 | tf_op jit(solution)/shard_map/ppermute | solution.py:20
  12.3 14.9 %collective-permute-done.2.refs_1_ = bf16[512,1024]{1,0:T(8,128)(2,1)S(1)} collective-permute-done((bf16[512,1024]{1,0:T(8,128)(2,1)}, bf16[512,1024]{1,0:T(8,128)(2,1)S(1)}, u32[]{:S(2)}, u32[]{:S(2)}) %collective-permute-start.2) | collective-permute-done | bytes 1048608 | tf_op jit(solution)/shard_map/ppermute | solution.py:26
  27.2 1.3 %collective-permute-start.9 = (bf16[512,1024]{1,0:T(8,128)(2,1)S(1)}, bf16[512,1024]{1,0:T(8,128)(2,1)S(1)}, u32[]{:S(2)}, u32[]{:S(2)}) collective-permute-start(bf16[512,1024]{1,0:T(8,128)(2,1)S(1)} %collective-permute-done.2.refs_1_), channel_id=1, source_target_pairs={{0,2},{2,4},{4,6},{6,8},{8,10},{10,12},{12,14},{14,16},{16,18},{18... | collective-permute-start | bytes 3145736 | tf_op jit(solution)/shard_map/ppermute | solution.py:20
  28.5 9.9 %collective-permute-done.1.refs_0_.refs_2_.refs_1_ = bf16[512,512]{1,0:T(8,128)(2,1)S(1)} collective-permute-done((bf16[512,512]{1,0:T(8,128)(2,1)S(1)}, bf16[512,512]{1,0:T(8,128)(2,1)S(1)}, u32[]{:S(2)}, u32[]{:S(2)}) %collective-permute-start.1) | collective-permute-done | bytes 524320 | tf_op jit(solution)/shard_map/ppermute | solution.py:26
  38.4 2.1 %collective-permute-start.4 = (bf16[512,256]{1,0:T(8,128)(2,1)S(1)}, bf16[512,256]{1,0:T(8,128)(2,1)S(1)}, u32[]{:S(2)}, u32[]{:S(2)}) collective-permute-start(bf16[512,256]{1,0:T(8,128)(2,1)S(1)} %get-tuple-element.24.own_piece), channel_id=1, source_target_pairs={{0,1},{1,0},{2,3},{3,2},{4,5},{5,4},{6,7},{7,6},{8,9},{9,8},{10,11... | collective-permute-start | bytes 786440 | tf_op jit(solution)/shard_map/ppermute | solution.py:26
  40.5 1.3 %shard_map.65.first = bf16[512,1024]{1,0:T(8,128)(2,1)S(1)} custom-call(s32[1]{0:T(128)} %bitcast.1.me, bf16[512,1024]{1,0:T(8,128)(2,1)S(1)} %collective-permute-done.following, bf16[256,512]{1,0:T(8,128)(2,1)S(1)} %bitcast.9, bf16[512,512]{1,0:T(8,128)(2,1)S(1)} %collective-permute-done.1.refs_0_.refs_2_.refs_1_), custom_call_target="tpu_custom_call" | custom-call | flops 8388608 | bytes 45056 | tf_op jit(solution)/shard_map/pallas_call | solution.py:216
  41.8 3.6 %shard_map.66.left = bf16[512,1024]{1,0:T(8,128)(2,1)S(1)} custom-call(s32[1]{0:T(128)} %bitcast.1.me, bf16[512,1024]{1,0:T(8,128)(2,1)S(1)} %bitcast.17, bf16[512,1024]{1,0:T(8,128)(2,1)S(1)} %shard_map.65.first, bf16[256,512]{1,0:T(8,128)(2,1)S(1)} %bitcast.15, bf16[512,1024]{1,0:T(8,128)(2,1)S(1)} %bitcast.20, ...), custom_call_target="tpu_custom_call" | custom-call | flops 25165824 | bytes 94208 | tf_op jit(solution)/shard_map/pallas_call | solution.py:216
  45.4 4.3 %collective-permute-done.3.refs_0_ = bf16[512,512]{1,0:T(8,128)(2,1)S(1)} collective-permute-done((bf16[512,512]{1,0:T(8,128)(2,1)S(1)}, bf16[512,512]{1,0:T(8,128)(2,1)S(1)}, u32[]{:S(2)}, u32[]{:S(2)}) %collective-permute-start.3) | collective-permute-done | bytes 524320 | tf_op jit(solution)/shard_map/ppermute | solution.py:26
  49.6 1.2 %shard_map.67 = (bf16[512,512]{1,0:T(8,128)(2,1)S(1)}, bf16[512,512]{1,0:T(8,128)(2,1)S(1)}) custom-call(s32[1]{0:T(128)} %bitcast.1.me, bf16[512,1024]{1,0:T(8,128)(2,1)S(1)} %shard_map.66.left, bf16[256,512]{1,0:T(8,128)(2,1)S(1)} %bitcast.10, bf16[512,512]{1,0:T(8,128)(2,1)S(1)} %get-tuple-element.22.own_piece, ...), custom_call_target="tpu_custom_call" | custom-call | flops 12582912 | bytes 61440 | tf_op jit(solution)/shard_map/pallas_call | solution.py:216
  50.8 1.3 %collective-permute-start.6 = (bf16[512,512]{1,0:T(8,128)(2,1)S(1)}, bf16[512,512]{1,0:T(8,128)(2,1)S(1)}, u32[]{:S(2)}, u32[]{:S(2)}) collective-permute-start(bf16[512,512]{1,0:T(8,128)(2,1)S(1)} %get-tuple-element.28), channel_id=1, source_target_pairs={{0,2},{2,4},{4,6},{6,8},{8,10},{10,12},{12,14},{14,16},{16,18},{18... | collective-permute-start | bytes 1572872 | tf_op jit(solution)/shard_map/ppermute | solution.py:20
  52.1 3.1 %collective-permute-done.4.refs_0_ = bf16[512,256]{1,0:T(8,128)(2,1)S(1)} collective-permute-done((bf16[512,256]{1,0:T(8,128)(2,1)S(1)}, bf16[512,256]{1,0:T(8,128)(2,1)S(1)}, u32[]{:S(2)}, u32[]{:S(2)}) %collective-permute-start.4) | collective-permute-done | bytes 262176 | tf_op jit(solution)/shard_map/ppermute | solution.py:26
  55.3 1.0 %shard_map.68 = (bf16[512,256]{1,0:T(8,128)(2,1)S(1)}, bf16[512,256]{1,0:T(8,128)(2,1)S(1)}) custom-call(s32[1]{0:T(128)} %bitcast.1.me, bf16[512,1024]{1,0:T(8,128)(2,1)S(1)} %shard_map.66.left, bf16[256,512]{1,0:T(8,128)(2,1)S(1)} %bitcast.11, bf16[512,256]{1,0:T(8,128)(2,1)S(1)} %get-tuple-element.24.own_piece, ...), custom_call_target="tpu_custom_call" | custom-call | flops 6291456 | bytes 45056 | tf_op jit(solution)/shard_map/pallas_call | solution.py:216
  56.2 1.6 %collective-permute-start.7 = (bf16[512,256]{1,0:T(8,128)(2,1)S(1)}, bf16[512,256]{1,0:T(8,128)(2,1)S(1)}, u32[]{:S(2)}, u32[]{:S(2)}) collective-permute-start(bf16[512,256]{1,0:T(8,128)(2,1)S(1)} %get-tuple-element.29), channel_id=1, source_target_pairs={{0,2},{2,4},{4,6},{6,8},{8,10},{10,12},{12,14},{14,16},{16,18},{18... | collective-permute-start | bytes 786440 | tf_op jit(solution)/shard_map/ppermute | solution.py:20
  57.8 2.2 %collective-permute-done.5.refs_0_ = bf16[512,256]{1,0:T(8,128)(2,1)S(1)} collective-permute-done((bf16[512,256]{1,0:T(8,128)(2,1)S(1)}, bf16[512,256]{1,0:T(8,128)(2,1)S(1)}, u32[]{:S(2)}, u32[]{:S(2)}) %collective-permute-start.5) | collective-permute-done | bytes 262176 | tf_op jit(solution)/shard_map/ppermute | solution.py:26
  60.0 1.0 %shard_map.69 = (bf16[512,256]{1,0:T(8,128)(2,1)S(1)}, bf16[512,256]{1,0:T(8,128)(2,1)S(1)}) custom-call(s32[1]{0:T(128)} %bitcast.1.me, bf16[512,1024]{1,0:T(8,128)(2,1)S(1)} %shard_map.66.left, bf16[256,512]{1,0:T(8,128)(2,1)S(1)} %bitcast.12, bf16[512,256]{1,0:T(8,128)(2,1)S(1)} %get-tuple-element.26.own_piece, ...), custom_call_target="tpu_custom_call" | custom-call | flops 1610612736 | bytes 45056 | tf_op jit(solution)/shard_map/pallas_call | solution.py:216
  61.0 2.2 %collective-permute-start.10 = (bf16[512,256]{1,0:T(8,128)(2,1)S(1)}, bf16[512,256]{1,0:T(8,128)(2,1)S(1)}, u32[]{:S(2)}, u32[]{:S(2)}) collective-permute-start(bf16[512,256]{1,0:T(8,128)(2,1)S(1)} %get-tuple-element.30), channel_id=1, source_target_pairs={{0,2},{2,4},{4,6},{6,8},{8,10},{10,12},{12,14},{14,16},{16,18},{18... | collective-permute-start | bytes 786440 | tf_op jit(solution)/shard_map/ppermute | solution.py:20
  63.3 0.7 shard_map.71
  63.9 1.5 %collective-permute-start.12 = (bf16[160,1024]{1,0:T(8,128)(2,1)S(1)}, bf16[160,1024]{1,0:T(8,128)(2,1)S(1)}, u32[]{:S(2)}, u32[]{:S(2)}) collective-permute-start(bf16[160,1024]{1,0:T(8,128)(2,1)S(1)} %get-tuple-element.34), channel_id=1, source_target_pairs={{0,1},{1,0},{2,3},{3,2},{4,5},{5,4},{6,7},{7,6},{8,9},{9,8},{10,11... | collective-permute-start | bytes 983048 | tf_op jit(solution)/shard_map/ppermute | solution.py:33
  65.5 1.0 %shard_map.70.partial = f32[512,1024]{1,0:T(8,128)S(1)} custom-call(s32[1]{0:T(128)} %bitcast.1.me, bf16[512,512]{1,0:T(8,128)(2,1)S(1)} %get-tuple-element.23.refs_0_, bf16[512,256]{1,0:T(8,128)(2,1)S(1)} %get-tuple-element.25.refs_1_, bf16[512,256]{1,0:T(8,128)(2,1)S(1)} %get-tuple-element.27.refs_2_, bf16[512,512]{1,0:T(8,128)(2,1)S(1)} %collective-permute-done.6.refs_3_, ...), custom_call_target="tpu_custom_call" | custom-call | flops 805306368 | bytes 94208 | tf_op jit(solution)/shard_map/pallas_call | solution.py:216
  66.6 0.6 shard_map.72
  67.2 0.6 collective-permute-start.13
  67.8 1.5 %collective-permute-start.14 = (bf16[160,256]{1,0:T(8,128)(2,1)S(1)}, bf16[160,256]{1,0:T(8,128)(2,1)S(1)}, u32[]{:S(2)}, u32[]{:S(2)}) collective-permute-start(bf16[160,256]{1,0:T(8,128)(2,1)S(1)} %get-tuple-element.36), channel_id=1, source_target_pairs={{0,1},{1,0},{2,3},{3,2},{4,5},{5,4},{6,7},{7,6},{8,9},{9,8},{10,11... | collective-permute-start | bytes 245768 | tf_op jit(solution)/shard_map/ppermute | solution.py:33
  69.3 0.6 collective-permute-start.11
  69.8 10.3 %collective-permute-done.11.refs_0_ = f32[8,128]{1,0:T(8,128)S(1)} collective-permute-done((f32[8,128]{1,0:T(8,128)S(1)}, f32[8,128]{1,0:T(8,128)S(1)}, u32[]{:S(2)}, u32[]{:S(2)}) %collective-permute-start.11) | collective-permute-done | bytes 4128 | tf_op jit(solution)/shard_map/ppermute | solution.py:33
  80.2 1.4 %shard_map.73 = f32[256,1024]{1,0:T(8,128)} custom-call(f32[256,1024]{1,0:T(8,128)S(1)} %bitcast.21, f32[8,128]{1,0:T(8,128)S(1)} %get-tuple-element.32.squares, f32[256,1024]{1,0:T(8,128)S(1)} %get-tuple-element.33.own, bf16[1024,256]{1,0:T(8,128)(2,1)S(1)} %get-tuple-element.31.right_last, f32[8,128]{1,0:T(8,128)S(1)} %collective-permute-done.11.refs_0_, ...), custom_call_target="tpu_custom_call" | custom-call | flops 1048576 | bytes 66944 | tf_op jit(solution)/shard_map/pallas_call | solution.py:216
  (22 shorter events, 0.2 us)
Async XLA Ops:
  0.0 27.2 %collective-permute-start.2 = (bf16[512,1024]{1,0:T(8,128)(2,1)}, bf16[512,1024]{1,0:T(8,128)(2,1)S(1)}, u32[]{:S(2)}, u32[]{:S(2)}) collective-permute-start(bf16[512,1024]{1,0:T(8,128)(2,1)} %bitcast.18), channel_id=1, source_target_pairs={{0,1},{1,0},{2,3},{3,2},{4,5},{5,4},{6,7},{7,6},{8,9},{9,8},{10,11... | collective-permute-start | bytes 3145736 | tf_op jit(solution)/shard_map/ppermute | solution.py:26
  3.0 37.5 %collective-permute-start = (bf16[512,1024]{1,0:T(8,128)(2,1)}, bf16[512,1024]{1,0:T(8,128)(2,1)S(1)}, u32[]{:S(2)}, u32[]{:S(2)}) collective-permute-start(bf16[512,1024]{1,0:T(8,128)(2,1)} %bitcast.16), channel_id=1, source_target_pairs={{2,0},{4,2},{6,4},{8,6},{10,8},{12,10},{14,12},{16,14},{18,16},{20... | collective-permute-start | bytes 3145736 | tf_op jit(solution)/shard_map/ppermute | solution.py:20
  4.3 1.0 %copy-start = (bf16[1,256,512]{2,1,0:T(8,128)(2,1)S(1)}, bf16[1,256,512]{2,1,0:T(8,128)(2,1)}, u32[]{:S(2)}) copy-start(bf16[1,256,512]{2,1,0:T(8,128)(2,1)} %param.9) | copy-start | bytes 786436
  5.2 1.2 %copy-start.2 = (bf16[1,512,1024]{2,1,0:T(8,128)(2,1)S(1)}, bf16[1,512,1024]{2,1,0:T(8,128)(2,1)}, u32[]{:S(2)}) copy-start(bf16[1,512,1024]{2,1,0:T(8,128)(2,1)} %param.8) | copy-start | bytes 3145732
  6.4 0.9 %copy-start.3 = (bf16[1,256,512]{2,1,0:T(8,128)(2,1)S(1)}, bf16[1,256,512]{2,1,0:T(8,128)(2,1)}, u32[]{:S(2)}) copy-start(bf16[1,256,512]{2,1,0:T(8,128)(2,1)} %param.7) | copy-start | bytes 786436
  7.4 34.4 %copy-start.4 = (bf16[1,1,512,1024]{3,2,1,0:T(8,128)(2,1)S(1)}, bf16[1,1,512,1024]{3,2,1,0:T(8,128)(2,1)}, u32[]{:S(2)}) copy-start(bf16[1,1,512,1024]{3,2,1,0:T(8,128)(2,1)} %param.6) | copy-start | bytes 3145732
  7.4 34.4 %copy-start.5 = (bf16[1,512,1024]{2,1,0:T(8,128)(2,1)S(1)}, bf16[1,512,1024]{2,1,0:T(8,128)(2,1)}, u32[]{:S(2)}) copy-start(bf16[1,512,1024]{2,1,0:T(8,128)(2,1)} %param.10) | copy-start | bytes 3145732
  7.6 30.8 %collective-permute-start.1 = (bf16[512,512]{1,0:T(8,128)(2,1)S(1)}, bf16[512,512]{1,0:T(8,128)(2,1)S(1)}, u32[]{:S(2)}, u32[]{:S(2)}) collective-permute-start(bf16[512,512]{1,0:T(8,128)(2,1)S(1)} %get-tuple-element.21), channel_id=1, source_target_pairs={{0,1},{1,0},{2,3},{3,2},{4,5},{5,4},{6,7},{7,6},{8,9},{9,8},{10,11... | collective-permute-start | bytes 1572872 | tf_op jit(solution)/shard_map/ppermute | solution.py:26
  7.7 41.9 %collective-permute-start.3 = (bf16[512,512]{1,0:T(8,128)(2,1)S(1)}, bf16[512,512]{1,0:T(8,128)(2,1)S(1)}, u32[]{:S(2)}, u32[]{:S(2)}) collective-permute-start(bf16[512,512]{1,0:T(8,128)(2,1)S(1)} %get-tuple-element.22.own_piece), channel_id=1, source_target_pairs={{0,1},{1,0},{2,3},{3,2},{4,5},{5,4},{6,7},{7,6},{8,9},{9,8},{10,11... | collective-permute-start | bytes 1572872 | tf_op jit(solution)/shard_map/ppermute | solution.py:26
  9.7 53.5 %collective-permute-start.8 = (bf16[512,1024]{1,0:T(8,128)(2,1)}, bf16[512,1024]{1,0:T(8,128)(2,1)S(1)}, u32[]{:S(2)}, u32[]{:S(2)}) collective-permute-start(bf16[512,1024]{1,0:T(8,128)(2,1)} %bitcast.19), channel_id=1, source_target_pairs={{0,2},{2,4},{4,6},{6,8},{8,10},{10,12},{12,14},{14,16},{16,18},{18... | collective-permute-start | bytes 3145736 | tf_op jit(solution)/shard_map/ppermute | solution.py:20
  27.2 36.1 %collective-permute-start.9 = (bf16[512,1024]{1,0:T(8,128)(2,1)S(1)}, bf16[512,1024]{1,0:T(8,128)(2,1)S(1)}, u32[]{:S(2)}, u32[]{:S(2)}) collective-permute-start(bf16[512,1024]{1,0:T(8,128)(2,1)S(1)} %collective-permute-done.2.refs_1_), channel_id=1, source_target_pairs={{0,2},{2,4},{4,6},{6,8},{8,10},{10,12},{12,14},{14,16},{16,18},{18... | collective-permute-start | bytes 3145736 | tf_op jit(solution)/shard_map/ppermute | solution.py:20
  38.4 16.9 %collective-permute-start.4 = (bf16[512,256]{1,0:T(8,128)(2,1)S(1)}, bf16[512,256]{1,0:T(8,128)(2,1)S(1)}, u32[]{:S(2)}, u32[]{:S(2)}) collective-permute-start(bf16[512,256]{1,0:T(8,128)(2,1)S(1)} %get-tuple-element.24.own_piece), channel_id=1, source_target_pairs={{0,1},{1,0},{2,3},{3,2},{4,5},{5,4},{6,7},{7,6},{8,9},{9,8},{10,11... | collective-permute-start | bytes 786440 | tf_op jit(solution)/shard_map/ppermute | solution.py:26
  40.5 19.6 %collective-permute-start.5 = (bf16[512,256]{1,0:T(8,128)(2,1)S(1)}, bf16[512,256]{1,0:T(8,128)(2,1)S(1)}, u32[]{:S(2)}, u32[]{:S(2)}) collective-permute-start(bf16[512,256]{1,0:T(8,128)(2,1)S(1)} %get-tuple-element.26.own_piece), channel_id=1, source_target_pairs={{0,1},{1,0},{2,3},{3,2},{4,5},{5,4},{6,7},{7,6},{8,9},{9,8},{10,11... | collective-permute-start | bytes 786440 | tf_op jit(solution)/shard_map/ppermute | solution.py:26
  41.8 7.8 %copy-start.1 = (bf16[1,256,512]{2,1,0:T(8,128)(2,1)S(1)}, bf16[1,256,512]{2,1,0:T(8,128)(2,1)}, u32[]{:S(2)}) copy-start(bf16[1,256,512]{2,1,0:T(8,128)(2,1)} %param.9) | copy-start | bytes 786436
  50.8 12.4 %collective-permute-start.6 = (bf16[512,512]{1,0:T(8,128)(2,1)S(1)}, bf16[512,512]{1,0:T(8,128)(2,1)S(1)}, u32[]{:S(2)}, u32[]{:S(2)}) collective-permute-start(bf16[512,512]{1,0:T(8,128)(2,1)S(1)} %get-tuple-element.28), channel_id=1, source_target_pairs={{0,2},{2,4},{4,6},{6,8},{8,10},{10,12},{12,14},{14,16},{16,18},{18... | collective-permute-start | bytes 1572872 | tf_op jit(solution)/shard_map/ppermute | solution.py:20
  56.2 7.0 %collective-permute-start.7 = (bf16[512,256]{1,0:T(8,128)(2,1)S(1)}, bf16[512,256]{1,0:T(8,128)(2,1)S(1)}, u32[]{:S(2)}, u32[]{:S(2)}) collective-permute-start(bf16[512,256]{1,0:T(8,128)(2,1)S(1)} %get-tuple-element.29), channel_id=1, source_target_pairs={{0,2},{2,4},{4,6},{6,8},{8,10},{10,12},{12,14},{14,16},{16,18},{18... | collective-permute-start | bytes 786440 | tf_op jit(solution)/shard_map/ppermute | solution.py:20
  61.0 5.5 %collective-permute-start.10 = (bf16[512,256]{1,0:T(8,128)(2,1)S(1)}, bf16[512,256]{1,0:T(8,128)(2,1)S(1)}, u32[]{:S(2)}, u32[]{:S(2)}) collective-permute-start(bf16[512,256]{1,0:T(8,128)(2,1)S(1)} %get-tuple-element.30), channel_id=1, source_target_pairs={{0,2},{2,4},{4,6},{6,8},{8,10},{10,12},{12,14},{14,16},{16,18},{18... | collective-permute-start | bytes 786440 | tf_op jit(solution)/shard_map/ppermute | solution.py:20
  63.9 16.2 %collective-permute-start.12 = (bf16[160,1024]{1,0:T(8,128)(2,1)S(1)}, bf16[160,1024]{1,0:T(8,128)(2,1)S(1)}, u32[]{:S(2)}, u32[]{:S(2)}) collective-permute-start(bf16[160,1024]{1,0:T(8,128)(2,1)S(1)} %get-tuple-element.34), channel_id=1, source_target_pairs={{0,1},{1,0},{2,3},{3,2},{4,5},{5,4},{6,7},{7,6},{8,9},{9,8},{10,11... | collective-permute-start | bytes 983048 | tf_op jit(solution)/shard_map/ppermute | solution.py:33
  66.5 13.6 %copy-start.6 = (f32[1,256,1024]{2,1,0:T(8,128)S(1)}, f32[1,256,1024]{2,1,0:T(8,128)}, u32[]{:S(2)}) copy-start(f32[1,256,1024]{2,1,0:T(8,128)} %param.11) | copy-start | bytes 3145732
  67.2 13.0 %collective-permute-start.13 = (bf16[96,1024]{1,0:T(8,128)(2,1)S(1)}, bf16[96,1024]{1,0:T(8,128)(2,1)S(1)}, u32[]{:S(2)}, u32[]{:S(2)}) collective-permute-start(bf16[96,1024]{1,0:T(8,128)(2,1)S(1)} %get-tuple-element.35), channel_id=1, source_target_pairs={{0,1},{1,0},{2,3},{3,2},{4,5},{5,4},{6,7},{7,6},{8,9},{9,8},{10,11... | collective-permute-start | bytes 589832 | tf_op jit(solution)/shard_map/ppermute | solution.py:33
  67.8 12.4 %collective-permute-start.14 = (bf16[160,256]{1,0:T(8,128)(2,1)S(1)}, bf16[160,256]{1,0:T(8,128)(2,1)S(1)}, u32[]{:S(2)}, u32[]{:S(2)}) collective-permute-start(bf16[160,256]{1,0:T(8,128)(2,1)S(1)} %get-tuple-element.36), channel_id=1, source_target_pairs={{0,1},{1,0},{2,3},{3,2},{4,5},{5,4},{6,7},{7,6},{8,9},{9,8},{10,11... | collective-permute-start | bytes 245768 | tf_op jit(solution)/shard_map/ppermute | solution.py:33
  69.3 10.9 %collective-permute-start.11 = (f32[8,128]{1,0:T(8,128)S(1)}, f32[8,128]{1,0:T(8,128)S(1)}, u32[]{:S(2)}, u32[]{:S(2)}) collective-permute-start(f32[8,128]{1,0:T(8,128)S(1)} %get-tuple-element.32.squares), channel_id=1, source_target_pairs={{0,1},{1,0},{2,3},{3,2},{4,5},{5,4},{6,7},{7,6},{8,9},{9,8},{10,11... | collective-permute-start | bytes 12296 | tf_op jit(solution)/shard_map/ppermute | solution.py:33
where the time goes:
time: 81.9 us; the launch traced here: 81.5 us
  waiting for transfers between devices  44.7 us (55%)
  starting transfers between devices  21.5 us (26%)
  Pallas kernels  11.9 us (15%)
  local copies, waits for them, and re-layouts  3.14 us (4%)
    ppermute x5, waiting for transfers between devices, from_peers(): lax.ppermute(value, axis, [(source, (source - step) % count) for source i...  34.4 us
    pallas_call x10, Pallas kernels, call(): pl.pallas_call(kernel, out_shape=outs, compiler_params=pltpu.CompilerPara...  11.9 us
    ppermute x4, waiting for transfers between devices, to_peer(): lax.ppermute(value, axis, [(source, (source + step) % count) for source i...  10.3 us
    ppermute x6, starting transfers between devices, passed_along(): lax.ppermute(value, axis, [(source, source + steps) for source in range(i...  10.2 us
    ppermute x5, starting transfers between devices, from_peers(): lax.ppermute(value, axis, [(source, (source - step) % count) for source i...  7.14 us
    ppermute x4, starting transfers between devices, to_peer(): lax.ppermute(value, axis, [(source, (source + step) % count) for source i...  4.18 us
    unnamed x14, local copies, waits for them, and re-layouts  3.14 us
  transfers between devices with their start and end apart: 15, of which 6 were waited for; matrix products, arithmetic and copies ran while one was open for 0% of the time, Pallas kernels for 13%

commit v1 on v0

--- a/solution.py
+++ b/solution.py
@@ -7,7 +7,8 @@
 from jax.experimental.pallas import tpu as pltpu
 from jax.sharding import PartitionSpec as P
 
-SHARES = (2, 1, 1)
+SHARES = (3, 2, 2, 1)
+EARLY = 2
 ROWS = 16
 TILE = 256
 HALF = jnp.bfloat16
@@ -76,7 +77,7 @@
 
 
 def left_kernel(count, me, grads, first, inv_own, *refs):
-    rights, others, out = refs[:count], refs[count : 2 * count - 1], refs[2 * count - 1]
+    rights, others, out = refs[:count], refs[count : 2 * count - 1], refs[-1]
     depth, rows = rights[0].shape[0], inv_own.shape[0]
 
     @pl.loop(0, out.shape[1] // TILE)
@@ -118,9 +119,9 @@
 
 def early_kernel(count, rows, me, *refs):
     total = len(SHARES)
-    preconds, backs = refs[:total], refs[total : 2 * total - 1]
-    rights = refs[2 * total - 1 : 2 * total - 1 + count]
-    nears, (right_last, staged, stacked) = refs[2 * total - 1 + count : -3], refs[-3:]
+    preconds, backs = refs[:total], refs[total : total + EARLY]
+    rights = refs[total + EARLY : total + EARLY + count]
+    nears, (right_last, staged, stacked) = refs[total + EARLY + count : -3], refs[-3:]
     depth, known, near = rights[0].shape[0], stacked.shape[1], staged.shape[0]
     for row_step in range(1, count):
         start = lax.rem(me[0] + row_step, count) * rows
@@ -153,17 +154,20 @@
             partial[here, columns] = staged[here, columns].astype(FULL) - product
 
 
-def update_kernel(count, me, partial, back, right_last, *refs):
+def update_kernel(count, me, partial, right_last, *refs):
+    backs, refs = refs[: len(SHARES) - EARLY], refs[len(SHARES) - EARLY :]
     squares, own = refs[:2]
     fars, rests = refs[2 : count + 1], refs[count + 1 :]
     rows, wide = own.shape
+    back = backs[-1]
+    late = right_last.shape[1] - back.shape[1]
     total = jnp.zeros((), FULL)
     for step in range(count):
         here = span(me, step, count, rows)
         for start in range(0, wide, TILE):
             columns = slice(start, start + TILE)
             update = partial[here, columns] - dot(
-                back[here, :], right_last[columns, :], ((1,), (1,))
+                back[here, :], right_last[columns, late:], ((1,), (1,))
             )
             total += jnp.sum(update * update)
             if step == 0:
@@ -174,7 +178,7 @@
         if step:
             start = lax.rem(me[0] + step, count) * rows
             lines = pl.ds(pl.multiple_of(start, ROWS), rests[step - 1].shape[0])
-            rests[step - 1][...] = back[lines, :]
+            stack(rests[step - 1], backs, lines)
     squares[...] = jnp.full(squares.shape, total, FULL)
 
 
@@ -207,10 +211,11 @@
         copy.wait()
 
 
-def call(kernel, outs, operands, flops, **options):
+def call(kernel, outs, operands, flops, unread=(), **options):
     moved = sum(value.size * value.dtype.itemsize for value in (*operands, *outs))
     vmem = pl.BlockSpec(memory_space=pltpu.VMEM)
     specs = [pl.BlockSpec(memory_space=pltpu.SMEM)] + [vmem] * (len(operands) - 1)
+    specs += [pl.BlockSpec(memory_space=pl.ANY)] * len(unread)
     settings = dict(in_specs=specs, out_specs=[vmem] * len(outs))
     settings.update(options)
     return pl.pallas_call(
@@ -219,7 +224,7 @@
         compiler_params=pltpu.CompilerParams(vmem_limit_bytes=16 * 1024 * 1024),
         cost_estimate=pl.CostEstimate(flops=flops, bytes_accessed=moved // 64, transcendentals=0),
         **settings,
-    )(*operands)
+    )(*operands, *unread)
 
 
 def body(gradients, inverse_out, inverse_in, cross_out, cross_in, momentum):
@@ -260,6 +265,7 @@
         [shape((tall, wide), HALF)],
         [me, own_block, first, inverse_out[0], *in_blocks, *pairs],
         tall * wide * (tall + wide) // 32,
+        unread=previous_blocks[:1],
     )
     preconds, backs = [], []
     for at, (piece, peers) in enumerate(zip(cuts, cut_peers)):
@@ -272,14 +278,14 @@
         )
         preconds.append(precond)
         backs.append(passed_along(back, "layer", 1))
-    near = 5 * rows // 8 // ROWS * ROWS
-    peers, last = count - 1, widths[-1]
+    near = 3 * rows // 4 // ROWS * ROWS
+    peers, last, later = count - 1, widths[-1], sum(widths[EARLY:])
     *nears, right_last = call(
         part(early_kernel, count, rows),
-        [shape((near, wide), HALF)] * peers + [shape((wide, last), HALF)],
-        [me, *preconds, *backs[:-1], *previous_blocks],
-        2 * peers * near * wide * (wide - last),
-        scratch_shapes=[pltpu.VMEM((near, wide), HALF), pltpu.VMEM((near, wide - last), HALF)],
+        [shape((near, wide), HALF)] * peers + [shape((wide, later), HALF)],
+        [me, *preconds, *backs[:EARLY], *previous_blocks],
+        2 * peers * near * wide * (wide - later),
+        scratch_shapes=[pltpu.VMEM((near, wide), HALF), pltpu.VMEM((near, wide - later), HALF)],
     )
     nears = [to_peer(value, "rep", at + 1) for at, value in enumerate(nears)]
     (partial,) = call(
@@ -293,8 +299,8 @@
         part(update_kernel, count),
         [shape((8, 128), FULL), shape((rows, wide), FULL)]
         + [shape((rows - near, wide), HALF)] * peers
-        + [shape((near, last), HALF)] * peers,
-        [me, partial, backs[-1], right_last],
+        + [shape((near, later), HALF)] * peers,
+        [me, partial, right_last, *backs[EARLY:]],
         2 * tall * wide * last,
     )
     sends = [to_peer(value, "rep", at % peers + 1) for at, value in enumerate(sends)]

time: 81.9 us -> 83.1 us (1.015)
  waiting for transfers between devices: 44.7 us -> 34.6 us
  starting transfers between devices: 21.5 us -> 31.5 us
  Pallas kernels: 11.9 us -> 13.2 us
    ppermute x5 -> x6, waiting for transfers between devices: 34.4 us -> 26.4 us  [from_peers(): lax.ppermute(value, axis, [(source, (source - step) % count) for source i...]
    ppermute x6 -> x7, starting transfers between devices: 10.2 us -> 17.1 us  [passed_along(): lax.ppermute(value, axis, [(source, source + steps) for source in range(i...]
    ppermute x5 -> x6, starting transfers between devices: 7.14 us -> 9.9 us  [from_peers(): lax.ppermute(value, axis, [(source, (source - step) % count) for source i...]
    ppermute x4, waiting for transfers between devices: 10.3 us -> 8.19 us  [to_peer(): lax.ppermute(value, axis, [(source, (source + step) % count) for source i...]
    pallas_call x10 -> x11, Pallas kernels: 11.9 us -> 13.2 us  [call(): pl.pallas_call(kernel, out_shape=outs, compiler_params=pltpu.CompilerPara...]
    unnamed x14 -> x16, local copies, waits for them, and re-layouts: 3.14 us -> 3.14 us
  transfers between devices with their start and end apart: 15 -> 17, of which waited for: 6 -> 6; matrix products, arithmetic and copies ran while one was open for 0% -> 0% of each run, Pallas kernels for 13% -> 14%
where the time goes in v1:
time: 83.1 us; the launch traced here: 82.7 us
  waiting for transfers between devices  34.6 us (42%)
  starting transfers between devices  31.5 us (38%)
  Pallas kernels  13.2 us (16%)
  local copies, waits for them, and re-layouts  3.14 us (4%)
    ppermute x6, waiting for transfers between devices, from_peers(): lax.ppermute(value, axis, [(source, (source - step) % count) for source i...  26.4 us
    ppermute x7, starting transfers between devices, passed_along(): lax.ppermute(value, axis, [(source, source + steps) for source in range(i...  17.1 us
    pallas_call x11, Pallas kernels, call(): pl.pallas_call(kernel, out_shape=outs, compiler_params=pltpu.CompilerPara...  13.2 us
    ppermute x6, starting transfers between devices, from_peers(): lax.ppermute(value, axis, [(source, (source - step) % count) for source i...  9.9 us
    ppermute x4, waiting for transfers between devices, to_peer(): lax.ppermute(value, axis, [(source, (source + step) % count) for source i...  8.19 us
    ppermute x4, starting transfers between devices, to_peer(): lax.ppermute(value, axis, [(source, (source + step) % count) for source i...  4.5 us
    unnamed x16, local copies, waits for them, and re-layouts  3.14 us
  transfers between devices with their start and end apart: 17, of which 6 were waited for; matrix products, arithmetic and copies ran while one was open for 0% of the time, Pallas kernels for 14%

profile of v1, /device:TPU:0, one launch (start us, length us, event | category | flops | bytes accessed | tf_op | source)
XLA Modules:
  0.0 82.7 jit_solution(1531091731301360669)
XLA Ops:
  0.0 3.0 %collective-permute-start.2 = (bf16[512,1024]{1,0:T(8,128)(2,1)}, bf16[512,1024]{1,0:T(8,128)(2,1)S(1)}, u32[]{:S(2)}, u32[]{:S(2)}) collective-permute-start(bf16[512,1024]{1,0:T(8,128)(2,1)} %bitcast.18), channel_id=1, source_target_pairs={{0,1},{1,0},{2,3},{3,2},{4,5},{5,4},{6,7},{7,6},{8,9},{9,8},{10,11... | collective-permute-start | bytes 3145736 | tf_op jit(solution)/shard_map/ppermute | solution.py:27
  3.0 1.3 %collective-permute-start = (bf16[512,1024]{1,0:T(8,128)(2,1)}, bf16[512,1024]{1,0:T(8,128)(2,1)S(1)}, u32[]{:S(2)}, u32[]{:S(2)}) collective-permute-start(bf16[512,1024]{1,0:T(8,128)(2,1)} %bitcast.16), channel_id=1, source_target_pairs={{2,0},{4,2},{6,4},{8,6},{10,8},{12,10},{14,12},{16,14},{18,16},{20... | collective-permute-start | bytes 3145736 | tf_op jit(solution)/shard_map/ppermute | solution.py:21
  4.3 3.1 %collective-permute-start.3 = (bf16[512,1024]{1,0:T(8,128)(2,1)}, bf16[512,1024]{1,0:T(8,128)(2,1)S(1)}, u32[]{:S(2)}, u32[]{:S(2)}) collective-permute-start(bf16[512,1024]{1,0:T(8,128)(2,1)} %bitcast.19), channel_id=1, source_target_pairs={{0,2},{2,4},{4,6},{6,8},{8,10},{10,12},{12,14},{14,16},{16,18},{18... | collective-permute-start | bytes 3145736 | tf_op jit(solution)/shard_map/ppermute | solution.py:21
  7.4 0.9 %copy-done = bf16[1,256,512]{2,1,0:T(8,128)(2,1)S(1)} copy-done((bf16[1,256,512]{2,1,0:T(8,128)(2,1)S(1)}, bf16[1,256,512]{2,1,0:T(8,128)(2,1)}, u32[]{:S(2)}) %copy-start) | copy-done | bytes 262168
  8.3 0.9 %copy-done.2 = bf16[1,256,512]{2,1,0:T(8,128)(2,1)S(1)} copy-done((bf16[1,256,512]{2,1,0:T(8,128)(2,1)S(1)}, bf16[1,256,512]{2,1,0:T(8,128)(2,1)}, u32[]{:S(2)}) %copy-start.2) | copy-done | bytes 262168
  9.3 1.2 %copy-done.6 = bf16[1,512,1024]{2,1,0:T(8,128)(2,1)S(1)} copy-done((bf16[1,512,1024]{2,1,0:T(8,128)(2,1)S(1)}, bf16[1,512,1024]{2,1,0:T(8,128)(2,1)}, u32[]{:S(2)}) %copy-start.6) | copy-done | bytes 1048600
  10.8 16.3 %collective-permute-done.2.refs_1_ = bf16[512,1024]{1,0:T(8,128)(2,1)S(1)} collective-permute-done((bf16[512,1024]{1,0:T(8,128)(2,1)}, bf16[512,1024]{1,0:T(8,128)(2,1)S(1)}, u32[]{:S(2)}, u32[]{:S(2)}) %collective-permute-start.2) | collective-permute-done | bytes 1048608 | tf_op jit(solution)/shard_map/ppermute | solution.py:27
  27.2 1.3 %collective-permute-start.11 = (bf16[512,1024]{1,0:T(8,128)(2,1)S(1)}, bf16[512,1024]{1,0:T(8,128)(2,1)S(1)}, u32[]{:S(2)}, u32[]{:S(2)}) collective-permute-start(bf16[512,1024]{1,0:T(8,128)(2,1)S(1)} %collective-permute-done.2.refs_1_), channel_id=1, source_target_pairs={{0,2},{2,4},{4,6},{6,8},{8,10},{10,12},{12,14},{14,16},{16,18},{18... | collective-permute-start | bytes 3145736 | tf_op jit(solution)/shard_map/ppermute | solution.py:21
  28.5 2.1 %collective-permute-start.4 = (bf16[512,384]{1,0:T(8,128)(2,1)S(1)}, bf16[512,384]{1,0:T(8,128)(2,1)S(1)}, u32[]{:S(2)}, u32[]{:S(2)}) collective-permute-start(bf16[512,384]{1,0:T(8,128)(2,1)S(1)} %get-tuple-element.25.own_piece), channel_id=1, source_target_pairs={{0,1},{1,0},{2,3},{3,2},{4,5},{5,4},{6,7},{7,6},{8,9},{9,8},{10,11... | collective-permute-start | bytes 1179656 | tf_op jit(solution)/shard_map/ppermute | solution.py:27
  30.6 7.8 %collective-permute-done.1.refs_0_.refs_2_.refs_1_ = bf16[512,512]{1,0:T(8,128)(2,1)S(1)} collective-permute-done((bf16[512,512]{1,0:T(8,128)(2,1)S(1)}, bf16[512,512]{1,0:T(8,128)(2,1)S(1)}, u32[]{:S(2)}, u32[]{:S(2)}) %collective-permute-start.1) | collective-permute-done | bytes 524320 | tf_op jit(solution)/shard_map/ppermute | solution.py:27
  38.4 2.1 %collective-permute-start.5 = (bf16[512,256]{1,0:T(8,128)(2,1)S(1)}, bf16[512,256]{1,0:T(8,128)(2,1)S(1)}, u32[]{:S(2)}, u32[]{:S(2)}) collective-permute-start(bf16[512,256]{1,0:T(8,128)(2,1)S(1)} %get-tuple-element.27.own_piece), channel_id=1, source_target_pairs={{0,1},{1,0},{2,3},{3,2},{4,5},{5,4},{6,7},{7,6},{8,9},{9,8},{10,11... | collective-permute-start | bytes 786440 | tf_op jit(solution)/shard_map/ppermute | solution.py:27
  40.5 1.3 %shard_map.65.first = bf16[512,1024]{1,0:T(8,128)(2,1)S(1)} custom-call(s32[1]{0:T(128)} %bitcast.1.me, bf16[512,1024]{1,0:T(8,128)(2,1)S(1)} %collective-permute-done.following, bf16[256,512]{1,0:T(8,128)(2,1)S(1)} %bitcast.9, bf16[512,512]{1,0:T(8,128)(2,1)S(1)} %collective-permute-done.1.refs_0_.refs_2_.refs_1_), custom_call_target="tpu_custom_call" | custom-call | flops 8388608 | bytes 45056 | tf_op jit(solution)/shard_map/pallas_call | solution.py:221
  41.8 3.6 %shard_map.66.left = bf16[512,1024]{1,0:T(8,128)(2,1)S(1)} custom-call(s32[1]{0:T(128)} %bitcast.1.me, bf16[512,1024]{1,0:T(8,128)(2,1)S(1)} %bitcast.17, bf16[512,1024]{1,0:T(8,128)(2,1)S(1)} %shard_map.65.first, bf16[256,512]{1,0:T(8,128)(2,1)S(1)} %bitcast.15, bf16[512,1024]{1,0:T(8,128)(2,1)S(1)} %bitcast.20, ...), custom_call_target="tpu_custom_call" | custom-call | flops 25165824 | bytes 94208 | tf_op jit(solution)/shard_map/pallas_call | solution.py:221
  45.4 1.5 %collective-permute-done.4.refs_0_ = bf16[512,384]{1,0:T(8,128)(2,1)S(1)} collective-permute-done((bf16[512,384]{1,0:T(8,128)(2,1)S(1)}, bf16[512,384]{1,0:T(8,128)(2,1)S(1)}, u32[]{:S(2)}, u32[]{:S(2)}) %collective-permute-start.4) | collective-permute-done | bytes 393248 | tf_op jit(solution)/shard_map/ppermute | solution.py:27
  46.8 1.2 %shard_map.67 = (bf16[512,384]{1,0:T(8,128)(2,1)S(1)}, bf16[512,384]{1,0:T(8,128)(2,1)S(1)}) custom-call(s32[1]{0:T(128)} %bitcast.1.me, bf16[512,1024]{1,0:T(8,128)(2,1)S(1)} %shard_map.66.left, bf16[256,512]{1,0:T(8,128)(2,1)S(1)} %bitcast.10, bf16[512,384]{1,0:T(8,128)(2,1)S(1)} %get-tuple-element.25.own_piece, ...), custom_call_target="tpu_custom_call" | custom-call | flops 9437184 | bytes 53248 | tf_op jit(solution)/shard_map/pallas_call | solution.py:221
  48.0 1.3 %collective-permute-start.8 = (bf16[512,384]{1,0:T(8,128)(2,1)S(1)}, bf16[512,384]{1,0:T(8,128)(2,1)S(1)}, u32[]{:S(2)}, u32[]{:S(2)}) collective-permute-start(bf16[512,384]{1,0:T(8,128)(2,1)S(1)} %get-tuple-element.33), channel_id=1, source_target_pairs={{0,2},{2,4},{4,6},{6,8},{8,10},{10,12},{12,14},{14,16},{16,18},{18... | collective-permute-start | bytes 1179656 | tf_op jit(solution)/shard_map/ppermute | solution.py:21
  49.3 2.1 %collective-permute-start.6 = (bf16[512,256]{1,0:T(8,128)(2,1)S(1)}, bf16[512,256]{1,0:T(8,128)(2,1)S(1)}, u32[]{:S(2)}, u32[]{:S(2)}) collective-permute-start(bf16[512,256]{1,0:T(8,128)(2,1)S(1)} %get-tuple-element.29.own_piece), channel_id=1, source_target_pairs={{0,1},{1,0},{2,3},{3,2},{4,5},{5,4},{6,7},{7,6},{8,9},{9,8},{10,11... | collective-permute-start | bytes 786440 | tf_op jit(solution)/shard_map/ppermute | solution.py:27
  51.6 1.0 %shard_map.68 = (bf16[512,256]{1,0:T(8,128)(2,1)S(1)}, bf16[512,256]{1,0:T(8,128)(2,1)S(1)}) custom-call(s32[1]{0:T(128)} %bitcast.1.me, bf16[512,1024]{1,0:T(8,128)(2,1)S(1)} %shard_map.66.left, bf16[256,512]{1,0:T(8,128)(2,1)S(1)} %bitcast.11, bf16[512,256]{1,0:T(8,128)(2,1)S(1)} %get-tuple-element.27.own_piece, ...), custom_call_target="tpu_custom_call" | custom-call | flops 6291456 | bytes 45056 | tf_op jit(solution)/shard_map/pallas_call | solution.py:221
  52.6 3.7 %collective-permute-start.9 = (bf16[512,256]{1,0:T(8,128)(2,1)S(1)}, bf16[512,256]{1,0:T(8,128)(2,1)S(1)}, u32[]{:S(2)}, u32[]{:S(2)}) collective-permute-start(bf16[512,256]{1,0:T(8,128)(2,1)S(1)} %get-tuple-element.34), channel_id=1, source_target_pairs={{0,2},{2,4},{4,6},{6,8},{8,10},{10,12},{12,14},{14,16},{16,18},{18... | collective-permute-start | bytes 786440 | tf_op jit(solution)/shard_map/ppermute | solution.py:21
  56.9 1.0 %shard_map.69 = (bf16[512,256]{1,0:T(8,128)(2,1)S(1)}, bf16[512,256]{1,0:T(8,128)(2,1)S(1)}) custom-call(s32[1]{0:T(128)} %bitcast.1.me, bf16[512,1024]{1,0:T(8,128)(2,1)S(1)} %shard_map.66.left, bf16[256,512]{1,0:T(8,128)(2,1)S(1)} %bitcast.12, bf16[512,256]{1,0:T(8,128)(2,1)S(1)} %get-tuple-element.29.own_piece, ...), custom_call_target="tpu_custom_call" | custom-call | flops 6291456 | bytes 45056 | tf_op jit(solution)/shard_map/pallas_call | solution.py:221
  57.9 3.5 %collective-permute-start.10 = (bf16[512,256]{1,0:T(8,128)(2,1)S(1)}, bf16[512,256]{1,0:T(8,128)(2,1)S(1)}, u32[]{:S(2)}, u32[]{:S(2)}) collective-permute-start(bf16[512,256]{1,0:T(8,128)(2,1)S(1)} %get-tuple-element.35), channel_id=1, source_target_pairs={{0,2},{2,4},{4,6},{6,8},{8,10},{10,12},{12,14},{14,16},{16,18},{18... | collective-permute-start | bytes 786440 | tf_op jit(solution)/shard_map/ppermute | solution.py:21
  61.3 0.7 collective-permute-done.7.refs_0_
  62.0 1.0 %shard_map.70 = (bf16[512,128]{1,0:T(8,128)(2,1)S(1)}, bf16[512,128]{1,0:T(8,128)(2,1)S(1)}) custom-call(s32[1]{0:T(128)} %bitcast.1.me, bf16[512,1024]{1,0:T(8,128)(2,1)S(1)} %shard_map.66.left, bf16[256,512]{1,0:T(8,128)(2,1)S(1)} %bitcast.13, bf16[512,128]{1,0:T(8,128)(2,1)S(1)} %get-tuple-element.31.own_piece, ...), custom_call_target="tpu_custom_call" | custom-call | flops 805306368 | bytes 36864 | tf_op jit(solution)/shard_map/pallas_call | solution.py:221
  63.0 0.6 shard_map.72
  63.7 1.8 %collective-permute-start.14 = (bf16[192,1024]{1,0:T(8,128)(2,1)S(1)}, bf16[192,1024]{1,0:T(8,128)(2,1)S(1)}, u32[]{:S(2)}, u32[]{:S(2)}) collective-permute-start(bf16[192,1024]{1,0:T(8,128)(2,1)S(1)} %get-tuple-element.40), channel_id=1, source_target_pairs={{0,1},{1,0},{2,3},{3,2},{4,5},{5,4},{6,7},{7,6},{8,9},{9,8},{10,11... | collective-permute-start | bytes 1179656 | tf_op jit(solution)/shard_map/ppermute | solution.py:34
  65.5 2.9 %collective-permute-start.12 = (bf16[512,128]{1,0:T(8,128)(2,1)S(1)}, bf16[512,128]{1,0:T(8,128)(2,1)S(1)}, u32[]{:S(2)}, u32[]{:S(2)}) collective-permute-start(bf16[512,128]{1,0:T(8,128)(2,1)S(1)} %get-tuple-element.37), channel_id=1, source_target_pairs={{0,2},{2,4},{4,6},{6,8},{8,10},{10,12},{12,14},{14,16},{16,18},{18... | collective-permute-start | bytes 393224 | tf_op jit(solution)/shard_map/ppermute | solution.py:21
  68.4 1.3 %shard_map.71.partial = f32[512,1024]{1,0:T(8,128)S(1)} custom-call(s32[1]{0:T(128)} %bitcast.1.me, bf16[512,384]{1,0:T(8,128)(2,1)S(1)} %get-tuple-element.26.refs_0_, bf16[512,256]{1,0:T(8,128)(2,1)S(1)} %get-tuple-element.28.refs_1_, bf16[512,256]{1,0:T(8,128)(2,1)S(1)} %get-tuple-element.30.refs_2_, bf16[512,128]{1,0:T(8,128)(2,1)S(1)} %get-tuple-element.32.refs_3_, ...), custom_call_target="tpu_custom_call" | custom-call | flops 939524096 | bytes 96256 | tf_op jit(solution)/shard_map/pallas_call | solution.py:221
  70.3 0.7 collective-permute-start.16
  71.0 1.4 %collective-permute-start.15 = (bf16[64,1024]{1,0:T(8,128)(2,1)S(1)}, bf16[64,1024]{1,0:T(8,128)(2,1)S(1)}, u32[]{:S(2)}, u32[]{:S(2)}) collective-permute-start(bf16[64,1024]{1,0:T(8,128)(2,1)S(1)} %get-tuple-element.41), channel_id=1, source_target_pairs={{0,1},{1,0},{2,3},{3,2},{4,5},{5,4},{6,7},{7,6},{8,9},{9,8},{10,11... | collective-permute-start | bytes 393224 | tf_op jit(solution)/shard_map/ppermute | solution.py:34
  72.4 0.6 collective-permute-start.13
  73.0 8.2 %collective-permute-done.13.refs_0_ = f32[8,128]{1,0:T(8,128)S(1)} collective-permute-done((f32[8,128]{1,0:T(8,128)S(1)}, f32[8,128]{1,0:T(8,128)S(1)}, u32[]{:S(2)}, u32[]{:S(2)}) %collective-permute-start.13) | collective-permute-done | bytes 4128 | tf_op jit(solution)/shard_map/ppermute | solution.py:34
  81.2 1.5 %shard_map.74 = f32[256,1024]{1,0:T(8,128)} custom-call(f32[256,1024]{1,0:T(8,128)S(1)} %bitcast.22, f32[8,128]{1,0:T(8,128)S(1)} %get-tuple-element.38.squares, f32[256,1024]{1,0:T(8,128)S(1)} %get-tuple-element.39.own, bf16[1024,384]{1,0:T(8,128)(2,1)S(1)} %get-tuple-element.36.right_last, f32[8,128]{1,0:T(8,128)S(1)} %collective-permute-done.13.refs_0_, ...), custom_call_target="tpu_custom_call" | custom-call | flops 1048576 | bytes 72064 | tf_op jit(solution)/shard_map/pallas_call | solution.py:221
  (29 shorter events, 1.7 us)
Async XLA Ops:
  0.0 27.2 %collective-permute-start.2 = (bf16[512,1024]{1,0:T(8,128)(2,1)}, bf16[512,1024]{1,0:T(8,128)(2,1)S(1)}, u32[]{:S(2)}, u32[]{:S(2)}) collective-permute-start(bf16[512,1024]{1,0:T(8,128)(2,1)} %bitcast.18), channel_id=1, source_target_pairs={{0,1},{1,0},{2,3},{3,2},{4,5},{5,4},{6,7},{7,6},{8,9},{9,8},{10,11... | collective-permute-start | bytes 3145736 | tf_op jit(solution)/shard_map/ppermute | solution.py:27
  3.0 37.5 %collective-permute-start = (bf16[512,1024]{1,0:T(8,128)(2,1)}, bf16[512,1024]{1,0:T(8,128)(2,1)S(1)}, u32[]{:S(2)}, u32[]{:S(2)}) collective-permute-start(bf16[512,1024]{1,0:T(8,128)(2,1)} %bitcast.16), channel_id=1, source_target_pairs={{2,0},{4,2},{6,4},{8,6},{10,8},{12,10},{14,12},{16,14},{18,16},{20... | collective-permute-start | bytes 3145736 | tf_op jit(solution)/shard_map/ppermute | solution.py:21
  4.3 37.5 %collective-permute-start.3 = (bf16[512,1024]{1,0:T(8,128)(2,1)}, bf16[512,1024]{1,0:T(8,128)(2,1)S(1)}, u32[]{:S(2)}, u32[]{:S(2)}) collective-permute-start(bf16[512,1024]{1,0:T(8,128)(2,1)} %bitcast.19), channel_id=1, source_target_pairs={{0,2},{2,4},{4,6},{6,8},{8,10},{10,12},{12,14},{14,16},{16,18},{18... | collective-permute-start | bytes 3145736 | tf_op jit(solution)/shard_map/ppermute | solution.py:21
  7.4 1.0 %copy-start = (bf16[1,256,512]{2,1,0:T(8,128)(2,1)S(1)}, bf16[1,256,512]{2,1,0:T(8,128)(2,1)}, u32[]{:S(2)}) copy-start(bf16[1,256,512]{2,1,0:T(8,128)(2,1)} %param.9) | copy-start | bytes 786436
  8.3 0.9 %copy-start.2 = (bf16[1,256,512]{2,1,0:T(8,128)(2,1)S(1)}, bf16[1,256,512]{2,1,0:T(8,128)(2,1)}, u32[]{:S(2)}) copy-start(bf16[1,256,512]{2,1,0:T(8,128)(2,1)} %param.7) | copy-start | bytes 786436
  9.3 1.2 %copy-start.6 = (bf16[1,512,1024]{2,1,0:T(8,128)(2,1)S(1)}, bf16[1,512,1024]{2,1,0:T(8,128)(2,1)}, u32[]{:S(2)}) copy-start(bf16[1,512,1024]{2,1,0:T(8,128)(2,1)} %param.8) | copy-start | bytes 3145732
  10.5 31.3 %copy-start.3 = (bf16[1,256,512]{2,1,0:T(8,128)(2,1)S(1)}, bf16[1,256,512]{2,1,0:T(8,128)(2,1)}, u32[]{:S(2)}) copy-start(bf16[1,256,512]{2,1,0:T(8,128)(2,1)} %param.7) | copy-start | bytes 786436
  10.5 31.3 %copy-start.4 = (bf16[1,1,512,1024]{3,2,1,0:T(8,128)(2,1)S(1)}, bf16[1,1,512,1024]{3,2,1,0:T(8,128)(2,1)}, u32[]{:S(2)}) copy-start(bf16[1,1,512,1024]{3,2,1,0:T(8,128)(2,1)} %param.6) | copy-start | bytes 3145732
  10.5 31.3 %copy-start.5 = (bf16[1,512,1024]{2,1,0:T(8,128)(2,1)S(1)}, bf16[1,512,1024]{2,1,0:T(8,128)(2,1)}, u32[]{:S(2)}) copy-start(bf16[1,512,1024]{2,1,0:T(8,128)(2,1)} %param.10) | copy-start | bytes 3145732
  10.8 27.6 %collective-permute-start.1 = (bf16[512,512]{1,0:T(8,128)(2,1)S(1)}, bf16[512,512]{1,0:T(8,128)(2,1)S(1)}, u32[]{:S(2)}, u32[]{:S(2)}) collective-permute-start(bf16[512,512]{1,0:T(8,128)(2,1)S(1)} %get-tuple-element.24), channel_id=1, source_target_pairs={{0,1},{1,0},{2,3},{3,2},{4,5},{5,4},{6,7},{7,6},{8,9},{9,8},{10,11... | collective-permute-start | bytes 1572872 | tf_op jit(solution)/shard_map/ppermute | solution.py:27
  27.2 35.9 %collective-permute-start.11 = (bf16[512,1024]{1,0:T(8,128)(2,1)S(1)}, bf16[512,1024]{1,0:T(8,128)(2,1)S(1)}, u32[]{:S(2)}, u32[]{:S(2)}) collective-permute-start(bf16[512,1024]{1,0:T(8,128)(2,1)S(1)} %collective-permute-done.2.refs_1_), channel_id=1, source_target_pairs={{0,2},{2,4},{4,6},{6,8},{8,10},{10,12},{12,14},{14,16},{16,18},{18... | collective-permute-start | bytes 3145736 | tf_op jit(solution)/shard_map/ppermute | solution.py:21
  28.5 18.3 %collective-permute-start.4 = (bf16[512,384]{1,0:T(8,128)(2,1)S(1)}, bf16[512,384]{1,0:T(8,128)(2,1)S(1)}, u32[]{:S(2)}, u32[]{:S(2)}) collective-permute-start(bf16[512,384]{1,0:T(8,128)(2,1)S(1)} %get-tuple-element.25.own_piece), channel_id=1, source_target_pairs={{0,1},{1,0},{2,3},{3,2},{4,5},{5,4},{6,7},{7,6},{8,9},{9,8},{10,11... | collective-permute-start | bytes 1179656 | tf_op jit(solution)/shard_map/ppermute | solution.py:27
  38.4 13.2 %collective-permute-start.5 = (bf16[512,256]{1,0:T(8,128)(2,1)S(1)}, bf16[512,256]{1,0:T(8,128)(2,1)S(1)}, u32[]{:S(2)}, u32[]{:S(2)}) collective-permute-start(bf16[512,256]{1,0:T(8,128)(2,1)S(1)} %get-tuple-element.27.own_piece), channel_id=1, source_target_pairs={{0,1},{1,0},{2,3},{3,2},{4,5},{5,4},{6,7},{7,6},{8,9},{9,8},{10,11... | collective-permute-start | bytes 786440 | tf_op jit(solution)/shard_map/ppermute | solution.py:27
  41.7 5.1 %copy-start.1 = (bf16[1,256,512]{2,1,0:T(8,128)(2,1)S(1)}, bf16[1,256,512]{2,1,0:T(8,128)(2,1)}, u32[]{:S(2)}) copy-start(bf16[1,256,512]{2,1,0:T(8,128)(2,1)} %param.9) | copy-start | bytes 786436
  48.0 15.0 %collective-permute-start.8 = (bf16[512,384]{1,0:T(8,128)(2,1)S(1)}, bf16[512,384]{1,0:T(8,128)(2,1)S(1)}, u32[]{:S(2)}, u32[]{:S(2)}) collective-permute-start(bf16[512,384]{1,0:T(8,128)(2,1)S(1)} %get-tuple-element.33), channel_id=1, source_target_pairs={{0,2},{2,4},{4,6},{6,8},{8,10},{10,12},{12,14},{14,16},{16,18},{18... | collective-permute-start | bytes 1179656 | tf_op jit(solution)/shard_map/ppermute | solution.py:21
  49.3 7.6 %collective-permute-start.6 = (bf16[512,256]{1,0:T(8,128)(2,1)S(1)}, bf16[512,256]{1,0:T(8,128)(2,1)S(1)}, u32[]{:S(2)}, u32[]{:S(2)}) collective-permute-start(bf16[512,256]{1,0:T(8,128)(2,1)S(1)} %get-tuple-element.29.own_piece), channel_id=1, source_target_pairs={{0,1},{1,0},{2,3},{3,2},{4,5},{5,4},{6,7},{7,6},{8,9},{9,8},{10,11... | collective-permute-start | bytes 786440 | tf_op jit(solution)/shard_map/ppermute | solution.py:27
  52.6 10.4 %collective-permute-start.9 = (bf16[512,256]{1,0:T(8,128)(2,1)S(1)}, bf16[512,256]{1,0:T(8,128)(2,1)S(1)}, u32[]{:S(2)}, u32[]{:S(2)}) collective-permute-start(bf16[512,256]{1,0:T(8,128)(2,1)S(1)} %get-tuple-element.34), channel_id=1, source_target_pairs={{0,2},{2,4},{4,6},{6,8},{8,10},{10,12},{12,14},{14,16},{16,18},{18... | collective-permute-start | bytes 786440 | tf_op jit(solution)/shard_map/ppermute | solution.py:21
  56.3 5.7 %collective-permute-start.7 = (bf16[512,128]{1,0:T(8,128)(2,1)S(1)}, bf16[512,128]{1,0:T(8,128)(2,1)S(1)}, u32[]{:S(2)}, u32[]{:S(2)}) collective-permute-start(bf16[512,128]{1,0:T(8,128)(2,1)S(1)} %get-tuple-element.31.own_piece), channel_id=1, source_target_pairs={{0,1},{1,0},{2,3},{3,2},{4,5},{5,4},{6,7},{7,6},{8,9},{9,8},{10,11... | collective-permute-start | bytes 393224 | tf_op jit(solution)/shard_map/ppermute | solution.py:27
  57.9 10.5 %collective-permute-start.10 = (bf16[512,256]{1,0:T(8,128)(2,1)S(1)}, bf16[512,256]{1,0:T(8,128)(2,1)S(1)}, u32[]{:S(2)}, u32[]{:S(2)}) collective-permute-start(bf16[512,256]{1,0:T(8,128)(2,1)S(1)} %get-tuple-element.35), channel_id=1, source_target_pairs={{0,2},{2,4},{4,6},{6,8},{8,10},{10,12},{12,14},{14,16},{16,18},{18... | collective-permute-start | bytes 786440 | tf_op jit(solution)/shard_map/ppermute | solution.py:21
  63.7 17.6 %collective-permute-start.14 = (bf16[192,1024]{1,0:T(8,128)(2,1)S(1)}, bf16[192,1024]{1,0:T(8,128)(2,1)S(1)}, u32[]{:S(2)}, u32[]{:S(2)}) collective-permute-start(bf16[192,1024]{1,0:T(8,128)(2,1)S(1)} %get-tuple-element.40), channel_id=1, source_target_pairs={{0,1},{1,0},{2,3},{3,2},{4,5},{5,4},{6,7},{7,6},{8,9},{9,8},{10,11... | collective-permute-start | bytes 1179656 | tf_op jit(solution)/shard_map/ppermute | solution.py:34
  65.5 4.3 %collective-permute-start.12 = (bf16[512,128]{1,0:T(8,128)(2,1)S(1)}, bf16[512,128]{1,0:T(8,128)(2,1)S(1)}, u32[]{:S(2)}, u32[]{:S(2)}) collective-permute-start(bf16[512,128]{1,0:T(8,128)(2,1)S(1)} %get-tuple-element.37), channel_id=1, source_target_pairs={{0,2},{2,4},{4,6},{6,8},{8,10},{10,12},{12,14},{14,16},{16,18},{18... | collective-permute-start | bytes 393224 | tf_op jit(solution)/shard_map/ppermute | solution.py:21
  69.7 11.5 %copy-start.7 = (f32[1,256,1024]{2,1,0:T(8,128)S(1)}, f32[1,256,1024]{2,1,0:T(8,128)}, u32[]{:S(2)}) copy-start(f32[1,256,1024]{2,1,0:T(8,128)} %param.11) | copy-start | bytes 3145732
  70.3 10.9 %collective-permute-start.16 = (bf16[192,384]{1,0:T(8,128)(2,1)S(1)}, bf16[192,384]{1,0:T(8,128)(2,1)S(1)}, u32[]{:S(2)}, u32[]{:S(2)}) collective-permute-start(bf16[192,384]{1,0:T(8,128)(2,1)S(1)} %get-tuple-element.42), channel_id=1, source_target_pairs={{0,1},{1,0},{2,3},{3,2},{4,5},{5,4},{6,7},{7,6},{8,9},{9,8},{10,11... | collective-permute-start | bytes 442376 | tf_op jit(solution)/shard_map/ppermute | solution.py:34
  71.0 10.2 %collective-permute-start.15 = (bf16[64,1024]{1,0:T(8,128)(2,1)S(1)}, bf16[64,1024]{1,0:T(8,128)(2,1)S(1)}, u32[]{:S(2)}, u32[]{:S(2)}) collective-permute-start(bf16[64,1024]{1,0:T(8,128)(2,1)S(1)} %get-tuple-element.41), channel_id=1, source_target_pairs={{0,1},{1,0},{2,3},{3,2},{4,5},{5,4},{6,7},{7,6},{8,9},{9,8},{10,11... | collective-permute-start | bytes 393224 | tf_op jit(solution)/shard_map/ppermute | solution.py:34
  72.4 8.8 %collective-permute-start.13 = (f32[8,128]{1,0:T(8,128)S(1)}, f32[8,128]{1,0:T(8,128)S(1)}, u32[]{:S(2)}, u32[]{:S(2)}) collective-permute-start(f32[8,128]{1,0:T(8,128)S(1)} %get-tuple-element.38.squares), channel_id=1, source_target_pairs={{0,1},{1,0},{2,3},{3,2},{4,5},{5,4},{6,7},{7,6},{8,9},{9,8},{10,11... | collective-permute-start | bytes 12296 | tf_op jit(solution)/shard_map/ppermute | solution.py:34

commit v2 on v0

--- a/solution.py
+++ b/solution.py
@@ -18,6 +18,11 @@
     count = lax.axis_size(axis)
     initial, last = (max(0, -steps), min(count, count - steps))
     return lax.ppermute(value, axis, [(source, source + steps) for source in range(initial, last)])
+
+
+def passed_round(value, axis):
+    count = lax.axis_size(axis)
+    return lax.ppermute(value, axis, [(source, (source + 1) % count) for source in range(count)])
 
 
 def from_peers(value, axis):
@@ -271,7 +276,7 @@
             weight * tall * piece.shape[1] * (tall + wide) // 32,
         )
         preconds.append(precond)
-        backs.append(passed_along(back, "layer", 1))
+        backs.append(passed_round(back, "layer"))
     near = 5 * rows // 8 // ROWS * ROWS
     peers, last = count - 1, widths[-1]
     *nears, right_last = call(

time: 81.9 us -> 81 us (0.989)
  starting transfers between devices: 21.5 us -> 18.4 us
  waiting for transfers between devices: 44.7 us -> 47.1 us
    ppermute x6 -> x3, starting transfers between devices: 10.2 us -> 5.15 us  [passed_along(): lax.ppermute(value, axis, [(source, source + steps) for source in range(i...]
    ppermute x4, waiting for transfers between devices: 10.3 us -> 5.37 us  [to_peer(): lax.ppermute(value, axis, [(source, (source + step) % count) for source i...]
    ppermute x0 -> x3, waiting for transfers between devices: none -> 4.6 us  [passed_round(): lax.ppermute(value, axis, [(source, (source + 1) % count) for source in r...]
    ppermute x5, waiting for transfers between devices: 34.4 us -> 37.2 us  [from_peers(): lax.ppermute(value, axis, [(source, (source - step) % count) for source i...]
    ppermute x4, starting transfers between devices: 4.18 us -> 5.93 us  [to_peer(): lax.ppermute(value, axis, [(source, (source + step) % count) for source i...]
  transfers between devices with their start and end apart: 15 -> 15, of which waited for: 6 -> 8; matrix products, arithmetic and copies ran while one was open for 0% -> 0% of each run, Pallas kernels for 13% -> 13%
where the time goes in v2:
time: 81 us; the launch traced here: 80.8 us
  waiting for transfers between devices  47.1 us (58%)
  starting transfers between devices  18.4 us (23%)
  Pallas kernels  11.9 us (15%)
  local copies, waits for them, and re-layouts  3.14 us (4%)
    ppermute x5, waiting for transfers between devices, from_peers(): lax.ppermute(value, axis, [(source, (source - step) % count) for source i...  37.2 us
    pallas_call x10, Pallas kernels, call(): pl.pallas_call(kernel, out_shape=outs, compiler_params=pltpu.CompilerPara...  11.9 us
    ppermute x5, starting transfers between devices, from_peers(): lax.ppermute(value, axis, [(source, (source - step) % count) for source i...  7.14 us
    ppermute x4, starting transfers between devices, to_peer(): lax.ppermute(value, axis, [(source, (source + step) % count) for source i...  5.93 us
    ppermute x4, waiting for transfers between devices, to_peer(): lax.ppermute(value, axis, [(source, (source + step) % count) for source i...  5.37 us
    ppermute x3, starting transfers between devices, passed_along(): lax.ppermute(value, axis, [(source, source + steps) for source in range(i...  5.15 us
    ppermute x3, waiting for transfers between devices, passed_round(): lax.ppermute(value, axis, [(source, (source + 1) % count) for source in r...  4.6 us
    unnamed x14, local copies, waits for them, and re-layouts  3.14 us
  transfers between devices with their start and end apart: 15, of which 8 were waited for; matrix products, arithmetic and copies ran while one was open for 0% of the time, Pallas kernels for 13%

profile of v2, /device:TPU:0, one launch (start us, length us, event | category | flops | bytes accessed | tf_op | source)
XLA Modules:
  0.0 80.8 jit_solution(12250642314137332111)
XLA Ops:
  0.0 3.0 %collective-permute-start.2 = (bf16[512,1024]{1,0:T(8,128)(2,1)}, bf16[512,1024]{1,0:T(8,128)(2,1)S(1)}, u32[]{:S(2)}, u32[]{:S(2)}) collective-permute-start(bf16[512,1024]{1,0:T(8,128)(2,1)} %bitcast.18), channel_id=1, source_target_pairs={{0,1},{1,0},{2,3},{3,2},{4,5},{5,4},{6,7},{7,6},{8,9},{9,8},{10,11... | collective-permute-start | bytes 3145736 | tf_op jit(solution)/shard_map/ppermute | solution.py:31
  3.0 1.3 %collective-permute-start = (bf16[512,1024]{1,0:T(8,128)(2,1)}, bf16[512,1024]{1,0:T(8,128)(2,1)S(1)}, u32[]{:S(2)}, u32[]{:S(2)}) collective-permute-start(bf16[512,1024]{1,0:T(8,128)(2,1)} %bitcast.16), channel_id=1, source_target_pairs={{2,0},{4,2},{6,4},{8,6},{10,8},{12,10},{14,12},{16,14},{18,16},{20... | collective-permute-start | bytes 3145736 | tf_op jit(solution)/shard_map/ppermute | solution.py:20
  4.3 0.9 %copy-done = bf16[1,256,512]{2,1,0:T(8,128)(2,1)S(1)} copy-done((bf16[1,256,512]{2,1,0:T(8,128)(2,1)S(1)}, bf16[1,256,512]{2,1,0:T(8,128)(2,1)}, u32[]{:S(2)}) %copy-start) | copy-done | bytes 262168
  5.2 1.2 %copy-done.2 = bf16[1,512,1024]{2,1,0:T(8,128)(2,1)S(1)} copy-done((bf16[1,512,1024]{2,1,0:T(8,128)(2,1)S(1)}, bf16[1,512,1024]{2,1,0:T(8,128)(2,1)}, u32[]{:S(2)}) %copy-start.2) | copy-done | bytes 1048600
  6.4 0.9 %copy-done.3 = bf16[1,256,512]{2,1,0:T(8,128)(2,1)S(1)} copy-done((bf16[1,256,512]{2,1,0:T(8,128)(2,1)S(1)}, bf16[1,256,512]{2,1,0:T(8,128)(2,1)}, u32[]{:S(2)}) %copy-start.3) | copy-done | bytes 262168
  7.4 0.2 shard_map.64
  7.6 0.1 collective-permute-start.1
  7.7 2.0 %collective-permute-start.3 = (bf16[512,512]{1,0:T(8,128)(2,1)S(1)}, bf16[512,512]{1,0:T(8,128)(2,1)S(1)}, u32[]{:S(2)}, u32[]{:S(2)}) collective-permute-start(bf16[512,512]{1,0:T(8,128)(2,1)S(1)} %get-tuple-element.22.own_piece), channel_id=1, source_target_pairs={{0,1},{1,0},{2,3},{3,2},{4,5},{5,4},{6,7},{7,6},{8,9},{9,8},{10,11... | collective-permute-start | bytes 1572872 | tf_op jit(solution)/shard_map/ppermute | solution.py:31
  9.7 2.5 %collective-permute-start.8 = (bf16[512,1024]{1,0:T(8,128)(2,1)}, bf16[512,1024]{1,0:T(8,128)(2,1)S(1)}, u32[]{:S(2)}, u32[]{:S(2)}) collective-permute-start(bf16[512,1024]{1,0:T(8,128)(2,1)} %bitcast.19), channel_id=1, source_target_pairs={{0,2},{2,4},{4,6},{6,8},{8,10},{10,12},{12,14},{14,16},{16,18},{18... | collective-permute-start | bytes 3145736 | tf_op jit(solution)/shard_map/ppermute | solution.py:20
  12.3 14.9 %collective-permute-done.2.refs_1_ = bf16[512,1024]{1,0:T(8,128)(2,1)S(1)} collective-permute-done((bf16[512,1024]{1,0:T(8,128)(2,1)}, bf16[512,1024]{1,0:T(8,128)(2,1)S(1)}, u32[]{:S(2)}, u32[]{:S(2)}) %collective-permute-start.2) | collective-permute-done | bytes 1048608 | tf_op jit(solution)/shard_map/ppermute | solution.py:31
  27.2 1.3 %collective-permute-start.9 = (bf16[512,1024]{1,0:T(8,128)(2,1)S(1)}, bf16[512,1024]{1,0:T(8,128)(2,1)S(1)}, u32[]{:S(2)}, u32[]{:S(2)}) collective-permute-start(bf16[512,1024]{1,0:T(8,128)(2,1)S(1)} %collective-permute-done.2.refs_1_), channel_id=1, source_target_pairs={{0,2},{2,4},{4,6},{6,8},{8,10},{10,12},{12,14},{14,16},{16,18},{18... | collective-permute-start | bytes 3145736 | tf_op jit(solution)/shard_map/ppermute | solution.py:20
  28.5 9.9 %collective-permute-done.1.refs_0_.refs_2_.refs_1_ = bf16[512,512]{1,0:T(8,128)(2,1)S(1)} collective-permute-done((bf16[512,512]{1,0:T(8,128)(2,1)S(1)}, bf16[512,512]{1,0:T(8,128)(2,1)S(1)}, u32[]{:S(2)}, u32[]{:S(2)}) %collective-permute-start.1) | collective-permute-done | bytes 524320 | tf_op jit(solution)/shard_map/ppermute | solution.py:31
  38.4 2.1 %collective-permute-start.4 = (bf16[512,256]{1,0:T(8,128)(2,1)S(1)}, bf16[512,256]{1,0:T(8,128)(2,1)S(1)}, u32[]{:S(2)}, u32[]{:S(2)}) collective-permute-start(bf16[512,256]{1,0:T(8,128)(2,1)S(1)} %get-tuple-element.24.own_piece), channel_id=1, source_target_pairs={{0,1},{1,0},{2,3},{3,2},{4,5},{5,4},{6,7},{7,6},{8,9},{9,8},{10,11... | collective-permute-start | bytes 786440 | tf_op jit(solution)/shard_map/ppermute | solution.py:31
  40.5 1.3 %shard_map.65.first = bf16[512,1024]{1,0:T(8,128)(2,1)S(1)} custom-call(s32[1]{0:T(128)} %bitcast.1.me, bf16[512,1024]{1,0:T(8,128)(2,1)S(1)} %collective-permute-done.following, bf16[256,512]{1,0:T(8,128)(2,1)S(1)} %bitcast.9, bf16[512,512]{1,0:T(8,128)(2,1)S(1)} %collective-permute-done.1.refs_0_.refs_2_.refs_1_), custom_call_target="tpu_custom_call" | custom-call | flops 8388608 | bytes 45056 | tf_op jit(solution)/shard_map/pallas_call | solution.py:221
  41.8 3.6 %shard_map.66.left = bf16[512,1024]{1,0:T(8,128)(2,1)S(1)} custom-call(s32[1]{0:T(128)} %bitcast.1.me, bf16[512,1024]{1,0:T(8,128)(2,1)S(1)} %bitcast.17, bf16[512,1024]{1,0:T(8,128)(2,1)S(1)} %shard_map.65.first, bf16[256,512]{1,0:T(8,128)(2,1)S(1)} %bitcast.15, bf16[512,1024]{1,0:T(8,128)(2,1)S(1)} %bitcast.20, ...), custom_call_target="tpu_custom_call" | custom-call | flops 25165824 | bytes 94208 | tf_op jit(solution)/shard_map/pallas_call | solution.py:221
  45.4 4.3 %collective-permute-done.3.refs_0_ = bf16[512,512]{1,0:T(8,128)(2,1)S(1)} collective-permute-done((bf16[512,512]{1,0:T(8,128)(2,1)S(1)}, bf16[512,512]{1,0:T(8,128)(2,1)S(1)}, u32[]{:S(2)}, u32[]{:S(2)}) %collective-permute-start.3) | collective-permute-done | bytes 524320 | tf_op jit(solution)/shard_map/ppermute | solution.py:31
  49.6 1.2 %shard_map.67 = (bf16[512,512]{1,0:T(8,128)(2,1)S(1)}, bf16[512,512]{1,0:T(8,128)(2,1)S(1)}) custom-call(s32[1]{0:T(128)} %bitcast.1.me, bf16[512,1024]{1,0:T(8,128)(2,1)S(1)} %shard_map.66.left, bf16[256,512]{1,0:T(8,128)(2,1)S(1)} %bitcast.10, bf16[512,512]{1,0:T(8,128)(2,1)S(1)} %get-tuple-element.22.own_piece, ...), custom_call_target="tpu_custom_call" | custom-call | flops 12582912 | bytes 61440 | tf_op jit(solution)/shard_map/pallas_call | solution.py:221
  50.9 4.4 %collective-permute-done.4.refs_0_ = bf16[512,256]{1,0:T(8,128)(2,1)S(1)} collective-permute-done((bf16[512,256]{1,0:T(8,128)(2,1)S(1)}, bf16[512,256]{1,0:T(8,128)(2,1)S(1)}, u32[]{:S(2)}, u32[]{:S(2)}) %collective-permute-start.4) | collective-permute-done | bytes 262176 | tf_op jit(solution)/shard_map/ppermute | solution.py:31
  55.3 1.0 %shard_map.68 = (bf16[512,256]{1,0:T(8,128)(2,1)S(1)}, bf16[512,256]{1,0:T(8,128)(2,1)S(1)}) custom-call(s32[1]{0:T(128)} %bitcast.1.me, bf16[512,1024]{1,0:T(8,128)(2,1)S(1)} %shard_map.66.left, bf16[256,512]{1,0:T(8,128)(2,1)S(1)} %bitcast.11, bf16[512,256]{1,0:T(8,128)(2,1)S(1)} %get-tuple-element.24.own_piece, ...), custom_call_target="tpu_custom_call" | custom-call | flops 6291456 | bytes 45056 | tf_op jit(solution)/shard_map/pallas_call | solution.py:221
  56.3 3.7 %collective-permute-done.5.refs_0_ = bf16[512,256]{1,0:T(8,128)(2,1)S(1)} collective-permute-done((bf16[512,256]{1,0:T(8,128)(2,1)S(1)}, bf16[512,256]{1,0:T(8,128)(2,1)S(1)}, u32[]{:S(2)}, u32[]{:S(2)}) %collective-permute-start.5) | collective-permute-done | bytes 262176 | tf_op jit(solution)/shard_map/ppermute | solution.py:31
  60.0 1.0 %shard_map.69 = (bf16[512,256]{1,0:T(8,128)(2,1)S(1)}, bf16[512,256]{1,0:T(8,128)(2,1)S(1)}) custom-call(s32[1]{0:T(128)} %bitcast.1.me, bf16[512,1024]{1,0:T(8,128)(2,1)S(1)} %shard_map.66.left, bf16[256,512]{1,0:T(8,128)(2,1)S(1)} %bitcast.12, bf16[512,256]{1,0:T(8,128)(2,1)S(1)} %get-tuple-element.26.own_piece, ...), custom_call_target="tpu_custom_call" | custom-call | flops 1610612736 | bytes 45056 | tf_op jit(solution)/shard_map/pallas_call | solution.py:221
  61.1 3.9 %collective-permute-done.7.refs_4_ = bf16[512,256]{1,0:T(8,128)(2,1)S(1)} collective-permute-done((bf16[512,256]{1,0:T(8,128)(2,1)S(1)}, bf16[512,256]{1,0:T(8,128)(2,1)S(1)}, u32[]{:S(2)}, u32[]{:S(2)}) %collective-permute-start.7) | collective-permute-done | bytes 262176 | tf_op jit(solution)/shard_map/ppermute | solution.py:25
  65.0 0.7 shard_map.71
  65.6 2.1 %collective-permute-start.12 = (bf16[160,1024]{1,0:T(8,128)(2,1)S(1)}, bf16[160,1024]{1,0:T(8,128)(2,1)S(1)}, u32[]{:S(2)}, u32[]{:S(2)}) collective-permute-start(bf16[160,1024]{1,0:T(8,128)(2,1)S(1)} %get-tuple-element.34), channel_id=1, source_target_pairs={{0,1},{1,0},{2,3},{3,2},{4,5},{5,4},{6,7},{7,6},{8,9},{9,8},{10,11... | collective-permute-start | bytes 983048 | tf_op jit(solution)/shard_map/ppermute | solution.py:38
  67.8 1.0 %shard_map.70.partial = f32[512,1024]{1,0:T(8,128)S(1)} custom-call(s32[1]{0:T(128)} %bitcast.1.me, bf16[512,512]{1,0:T(8,128)(2,1)S(1)} %get-tuple-element.23.refs_0_, bf16[512,256]{1,0:T(8,128)(2,1)S(1)} %get-tuple-element.25.refs_1_, bf16[512,256]{1,0:T(8,128)(2,1)S(1)} %get-tuple-element.27.refs_2_, bf16[512,512]{1,0:T(8,128)(2,1)S(1)} %collective-permute-done.6.refs_3_, ...), custom_call_target="tpu_custom_call" | custom-call | flops 805306368 | bytes 94208 | tf_op jit(solution)/shard_map/pallas_call | solution.py:221
  68.8 0.7 collective-permute-done.10.back
  69.6 0.6 shard_map.72
  70.2 1.8 %collective-permute-start.13 = (bf16[96,1024]{1,0:T(8,128)(2,1)S(1)}, bf16[96,1024]{1,0:T(8,128)(2,1)S(1)}, u32[]{:S(2)}, u32[]{:S(2)}) collective-permute-start(bf16[96,1024]{1,0:T(8,128)(2,1)S(1)} %get-tuple-element.35), channel_id=1, source_target_pairs={{0,1},{1,0},{2,3},{3,2},{4,5},{5,4},{6,7},{7,6},{8,9},{9,8},{10,11... | collective-permute-start | bytes 589832 | tf_op jit(solution)/shard_map/ppermute | solution.py:38
  72.0 0.3 collective-permute-start.14
  72.3 1.7 %collective-permute-start.11 = (f32[8,128]{1,0:T(8,128)S(1)}, f32[8,128]{1,0:T(8,128)S(1)}, u32[]{:S(2)}, u32[]{:S(2)}) collective-permute-start(f32[8,128]{1,0:T(8,128)S(1)} %get-tuple-element.32.squares), channel_id=1, source_target_pairs={{0,1},{1,0},{2,3},{3,2},{4,5},{5,4},{6,7},{7,6},{8,9},{9,8},{10,11... | collective-permute-start | bytes 12296 | tf_op jit(solution)/shard_map/ppermute | solution.py:38
  74.0 5.4 %collective-permute-done.11.refs_0_ = f32[8,128]{1,0:T(8,128)S(1)} collective-permute-done((f32[8,128]{1,0:T(8,128)S(1)}, f32[8,128]{1,0:T(8,128)S(1)}, u32[]{:S(2)}, u32[]{:S(2)}) %collective-permute-start.11) | collective-permute-done | bytes 4128 | tf_op jit(solution)/shard_map/ppermute | solution.py:38
  79.4 1.4 %shard_map.73 = f32[256,1024]{1,0:T(8,128)} custom-call(f32[256,1024]{1,0:T(8,128)S(1)} %bitcast.21, f32[8,128]{1,0:T(8,128)S(1)} %get-tuple-element.32.squares, f32[256,1024]{1,0:T(8,128)S(1)} %get-tuple-element.33.own, bf16[1024,256]{1,0:T(8,128)(2,1)S(1)} %get-tuple-element.31.right_last, f32[8,128]{1,0:T(8,128)S(1)} %collective-permute-done.11.refs_0_, ...), custom_call_target="tpu_custom_call" | custom-call | flops 1048576 | bytes 66944 | tf_op jit(solution)/shard_map/pallas_call | solution.py:221
  (22 shorter events, 0.2 us)
Async XLA Ops:
  0.0 27.2 %collective-permute-start.2 = (bf16[512,1024]{1,0:T(8,128)(2,1)}, bf16[512,1024]{1,0:T(8,128)(2,1)S(1)}, u32[]{:S(2)}, u32[]{:S(2)}) collective-permute-start(bf16[512,1024]{1,0:T(8,128)(2,1)} %bitcast.18), channel_id=1, source_target_pairs={{0,1},{1,0},{2,3},{3,2},{4,5},{5,4},{6,7},{7,6},{8,9},{9,8},{10,11... | collective-permute-start | bytes 3145736 | tf_op jit(solution)/shard_map/ppermute | solution.py:31
  3.0 37.5 %collective-permute-start = (bf16[512,1024]{1,0:T(8,128)(2,1)}, bf16[512,1024]{1,0:T(8,128)(2,1)S(1)}, u32[]{:S(2)}, u32[]{:S(2)}) collective-permute-start(bf16[512,1024]{1,0:T(8,128)(2,1)} %bitcast.16), channel_id=1, source_target_pairs={{2,0},{4,2},{6,4},{8,6},{10,8},{12,10},{14,12},{16,14},{18,16},{20... | collective-permute-start | bytes 3145736 | tf_op jit(solution)/shard_map/ppermute | solution.py:20
  4.3 1.0 %copy-start = (bf16[1,256,512]{2,1,0:T(8,128)(2,1)S(1)}, bf16[1,256,512]{2,1,0:T(8,128)(2,1)}, u32[]{:S(2)}) copy-start(bf16[1,256,512]{2,1,0:T(8,128)(2,1)} %param.9) | copy-start | bytes 786436
  5.2 1.2 %copy-start.2 = (bf16[1,512,1024]{2,1,0:T(8,128)(2,1)S(1)}, bf16[1,512,1024]{2,1,0:T(8,128)(2,1)}, u32[]{:S(2)}) copy-start(bf16[1,512,1024]{2,1,0:T(8,128)(2,1)} %param.8) | copy-start | bytes 3145732
  6.4 0.9 %copy-start.3 = (bf16[1,256,512]{2,1,0:T(8,128)(2,1)S(1)}, bf16[1,256,512]{2,1,0:T(8,128)(2,1)}, u32[]{:S(2)}) copy-start(bf16[1,256,512]{2,1,0:T(8,128)(2,1)} %param.7) | copy-start | bytes 786436
  7.4 34.4 %copy-start.4 = (bf16[1,1,512,1024]{3,2,1,0:T(8,128)(2,1)S(1)}, bf16[1,1,512,1024]{3,2,1,0:T(8,128)(2,1)}, u32[]{:S(2)}) copy-start(bf16[1,1,512,1024]{3,2,1,0:T(8,128)(2,1)} %param.6) | copy-start | bytes 3145732
  7.4 34.4 %copy-start.5 = (bf16[1,512,1024]{2,1,0:T(8,128)(2,1)S(1)}, bf16[1,512,1024]{2,1,0:T(8,128)(2,1)}, u32[]{:S(2)}) copy-start(bf16[1,512,1024]{2,1,0:T(8,128)(2,1)} %param.10) | copy-start | bytes 3145732
  7.6 30.8 %collective-permute-start.1 = (bf16[512,512]{1,0:T(8,128)(2,1)S(1)}, bf16[512,512]{1,0:T(8,128)(2,1)S(1)}, u32[]{:S(2)}, u32[]{:S(2)}) collective-permute-start(bf16[512,512]{1,0:T(8,128)(2,1)S(1)} %get-tuple-element.21), channel_id=1, source_target_pairs={{0,1},{1,0},{2,3},{3,2},{4,5},{5,4},{6,7},{7,6},{8,9},{9,8},{10,11... | collective-permute-start | bytes 1572872 | tf_op jit(solution)/shard_map/ppermute | solution.py:31
  7.7 41.9 %collective-permute-start.3 = (bf16[512,512]{1,0:T(8,128)(2,1)S(1)}, bf16[512,512]{1,0:T(8,128)(2,1)S(1)}, u32[]{:S(2)}, u32[]{:S(2)}) collective-permute-start(bf16[512,512]{1,0:T(8,128)(2,1)S(1)} %get-tuple-element.22.own_piece), channel_id=1, source_target_pairs={{0,1},{1,0},{2,3},{3,2},{4,5},{5,4},{6,7},{7,6},{8,9},{9,8},{10,11... | collective-permute-start | bytes 1572872 | tf_op jit(solution)/shard_map/ppermute | solution.py:31
  9.7 51.4 %collective-permute-start.8 = (bf16[512,1024]{1,0:T(8,128)(2,1)}, bf16[512,1024]{1,0:T(8,128)(2,1)S(1)}, u32[]{:S(2)}, u32[]{:S(2)}) collective-permute-start(bf16[512,1024]{1,0:T(8,128)(2,1)} %bitcast.19), channel_id=1, source_target_pairs={{0,2},{2,4},{4,6},{6,8},{8,10},{10,12},{12,14},{14,16},{16,18},{18... | collective-permute-start | bytes 3145736 | tf_op jit(solution)/shard_map/ppermute | solution.py:20
  27.2 37.8 %collective-permute-start.9 = (bf16[512,1024]{1,0:T(8,128)(2,1)S(1)}, bf16[512,1024]{1,0:T(8,128)(2,1)S(1)}, u32[]{:S(2)}, u32[]{:S(2)}) collective-permute-start(bf16[512,1024]{1,0:T(8,128)(2,1)S(1)} %collective-permute-done.2.refs_1_), channel_id=1, source_target_pairs={{0,2},{2,4},{4,6},{6,8},{8,10},{10,12},{12,14},{14,16},{16,18},{18... | collective-permute-start | bytes 3145736 | tf_op jit(solution)/shard_map/ppermute | solution.py:20
  38.4 16.9 %collective-permute-start.4 = (bf16[512,256]{1,0:T(8,128)(2,1)S(1)}, bf16[512,256]{1,0:T(8,128)(2,1)S(1)}, u32[]{:S(2)}, u32[]{:S(2)}) collective-permute-start(bf16[512,256]{1,0:T(8,128)(2,1)S(1)} %get-tuple-element.24.own_piece), channel_id=1, source_target_pairs={{0,1},{1,0},{2,3},{3,2},{4,5},{5,4},{6,7},{7,6},{8,9},{9,8},{10,11... | collective-permute-start | bytes 786440 | tf_op jit(solution)/shard_map/ppermute | solution.py:31
  40.5 19.6 %collective-permute-start.5 = (bf16[512,256]{1,0:T(8,128)(2,1)S(1)}, bf16[512,256]{1,0:T(8,128)(2,1)S(1)}, u32[]{:S(2)}, u32[]{:S(2)}) collective-permute-start(bf16[512,256]{1,0:T(8,128)(2,1)S(1)} %get-tuple-element.26.own_piece), channel_id=1, source_target_pairs={{0,1},{1,0},{2,3},{3,2},{4,5},{5,4},{6,7},{7,6},{8,9},{9,8},{10,11... | collective-permute-start | bytes 786440 | tf_op jit(solution)/shard_map/ppermute | solution.py:31
  41.8 7.8 %copy-start.1 = (bf16[1,256,512]{2,1,0:T(8,128)(2,1)S(1)}, bf16[1,256,512]{2,1,0:T(8,128)(2,1)}, u32[]{:S(2)}) copy-start(bf16[1,256,512]{2,1,0:T(8,128)(2,1)} %param.9) | copy-start | bytes 786436
  50.8 14.2 %collective-permute-start.6 = (bf16[512,512]{1,0:T(8,128)(2,1)S(1)}, bf16[512,512]{1,0:T(8,128)(2,1)S(1)}, u32[]{:S(2)}, u32[]{:S(2)}) collective-permute-start(bf16[512,512]{1,0:T(8,128)(2,1)S(1)} %get-tuple-element.28), channel_id=1, source_target_pairs={{0,2},{2,4},{4,6},{6,8},{8,10},{10,12},{12,14},{14,16},{16,18},{18... | collective-permute-start | bytes 1572872 | tf_op jit(solution)/shard_map/ppermute | solution.py:25
  56.2 8.7 %collective-permute-start.7 = (bf16[512,256]{1,0:T(8,128)(2,1)S(1)}, bf16[512,256]{1,0:T(8,128)(2,1)S(1)}, u32[]{:S(2)}, u32[]{:S(2)}) collective-permute-start(bf16[512,256]{1,0:T(8,128)(2,1)S(1)} %get-tuple-element.29), channel_id=1, source_target_pairs={{0,2},{2,4},{4,6},{6,8},{8,10},{10,12},{12,14},{14,16},{16,18},{18... | collective-permute-start | bytes 786440 | tf_op jit(solution)/shard_map/ppermute | solution.py:25
  61.0 8.5 %collective-permute-start.10 = (bf16[512,256]{1,0:T(8,128)(2,1)S(1)}, bf16[512,256]{1,0:T(8,128)(2,1)S(1)}, u32[]{:S(2)}, u32[]{:S(2)}) collective-permute-start(bf16[512,256]{1,0:T(8,128)(2,1)S(1)} %get-tuple-element.30), channel_id=1, source_target_pairs={{0,2},{2,4},{4,6},{6,8},{8,10},{10,12},{12,14},{14,16},{16,18},{18... | collective-permute-start | bytes 786440 | tf_op jit(solution)/shard_map/ppermute | solution.py:25
  65.6 13.7 %collective-permute-start.12 = (bf16[160,1024]{1,0:T(8,128)(2,1)S(1)}, bf16[160,1024]{1,0:T(8,128)(2,1)S(1)}, u32[]{:S(2)}, u32[]{:S(2)}) collective-permute-start(bf16[160,1024]{1,0:T(8,128)(2,1)S(1)} %get-tuple-element.34), channel_id=1, source_target_pairs={{0,1},{1,0},{2,3},{3,2},{4,5},{5,4},{6,7},{7,6},{8,9},{9,8},{10,11... | collective-permute-start | bytes 983048 | tf_op jit(solution)/shard_map/ppermute | solution.py:38
  68.8 10.5 %copy-start.6 = (f32[1,256,1024]{2,1,0:T(8,128)S(1)}, f32[1,256,1024]{2,1,0:T(8,128)}, u32[]{:S(2)}) copy-start(f32[1,256,1024]{2,1,0:T(8,128)} %param.11) | copy-start | bytes 3145732
  70.2 9.2 %collective-permute-start.13 = (bf16[96,1024]{1,0:T(8,128)(2,1)S(1)}, bf16[96,1024]{1,0:T(8,128)(2,1)S(1)}, u32[]{:S(2)}, u32[]{:S(2)}) collective-permute-start(bf16[96,1024]{1,0:T(8,128)(2,1)S(1)} %get-tuple-element.35), channel_id=1, source_target_pairs={{0,1},{1,0},{2,3},{3,2},{4,5},{5,4},{6,7},{7,6},{8,9},{9,8},{10,11... | collective-permute-start | bytes 589832 | tf_op jit(solution)/shard_map/ppermute | solution.py:38
  72.0 7.4 %collective-permute-start.14 = (bf16[160,256]{1,0:T(8,128)(2,1)S(1)}, bf16[160,256]{1,0:T(8,128)(2,1)S(1)}, u32[]{:S(2)}, u32[]{:S(2)}) collective-permute-start(bf16[160,256]{1,0:T(8,128)(2,1)S(1)} %get-tuple-element.36), channel_id=1, source_target_pairs={{0,1},{1,0},{2,3},{3,2},{4,5},{5,4},{6,7},{7,6},{8,9},{9,8},{10,11... | collective-permute-start | bytes 245768 | tf_op jit(solution)/shard_map/ppermute | solution.py:38
  72.3 7.1 %collective-permute-start.11 = (f32[8,128]{1,0:T(8,128)S(1)}, f32[8,128]{1,0:T(8,128)S(1)}, u32[]{:S(2)}, u32[]{:S(2)}) collective-permute-start(f32[8,128]{1,0:T(8,128)S(1)} %get-tuple-element.32.squares), channel_id=1, source_target_pairs={{0,1},{1,0},{2,3},{3,2},{4,5},{5,4},{6,7},{7,6},{8,9},{9,8},{10,11... | collective-permute-start | bytes 12296 | tf_op jit(solution)/shard_map/ppermute | solution.py:38
